TPU v7x, 512 devices: a whole 4x4x16 slice. The times are simulated.
512 devices in a mesh: dp: 4 (over x_lo, core), ctx: 16 (over z), tp: 8 (over x_hi, y).
Axes of the slice: x: 4 (x_hi: 2, x_lo: 2; x = x_hi * 2 + x_lo), y: 4, z: 16, core: 2. Of those that a mesh axis runs over, the one named last changes fastest.
Arguments:
- queries: bfloat16 [4, 2048, 3072], P('dp', 'ctx', 'tp'), may hold values from -40 to 40
- key_heads: bfloat16 [4, 2048, 1024], P('dp', 'ctx', 'tp'), may hold values from -40 to 40
- value_heads: bfloat16 [4, 2048, 1024], P('dp', 'ctx', 'tp'), may hold values from -6 to 6
- doc_ids: int32 [4, 2048], P('dp', 'ctx'), may hold values from 0 to 7, never falling along the last dimension, each value on 1 to 1152 neighbouring positions
- residual: bfloat16 [4, 2048, 3072], P('dp', 'ctx', 'tp'), may hold values from -12 to 12
- ln_gain: float32 [3072], P('tp'), may hold values from 0.1 to 1.9
- expert_ids: int32 [4, 2048, 4], P('dp', 'ctx'), may hold values from 0 to 15, all different within a row; in each aligned block of 128 rows (0 to 127, 128 to 255, ..., all dimensions but the last counted through in order) at most 33 rows name the same one
- expert_weight: float32 [4, 2048, 4], P('dp', 'ctx'), may hold values from 0.3 to 1
- w_gate: bfloat16 [16, 3072, 5376], P('ctx', 'dp', 'tp'), may hold values from -0.109375 to 0.109375
- w_up: bfloat16 [16, 3072, 5376], P('ctx', 'dp', 'tp'), may hold values from -0.109375 to 0.109375
- w_down: bfloat16 [16, 5376, 3072], P('ctx', 'tp', 'dp'), may hold values from -0.078125 to 0.078125
Outputs:
- mixed: bfloat16 [4, 2048, 3072], P('dp', 'ctx', 'tp')
Inputs may be any that keep to these rules, and one draw needn't show every extreme that they name: `doc_ids`: never falling along a row; each document holds at most 1152 positions and one holds exactly that many. `expert_ids`: each token names 4 different experts. Among the 128 tokens of one device no expert is named more than 33 times, a bound that some block reaches.
All inputs are finite; a program needn't handle non-finite values.
Results may differ from a plain program's by a relative error of at most 0.022.
Values may be sent and summed in bfloat16 or wider, within the bound.
No kernel may reach another device: no remote copies, remote signals or barrier semaphores. Data moves between devices by JAX's collectives and lax.ppermute only.
A program may use at most 64 MiB of HBM per device.

v0:
```python
import math

import jax
import jax.numpy as jnp
from jax import lax
from jax.sharding import PartitionSpec as P

HEAD_DIM = 128


def slot_table(route_block, expert_count, capacity):
    flat_ids = route_block.reshape(-1)
    onehot = (flat_ids[:, None] == jnp.arange(expert_count, dtype=jnp.int32)[None, :]).astype(
        jnp.int32
    )
    ranks = jnp.cumsum(onehot, axis=0) - 1
    placed = jnp.sum(onehot * ranks, axis=1)
    slot_of = flat_ids * capacity + placed
    token_ids = jnp.arange(flat_ids.shape[0], dtype=jnp.int32) // route_block.shape[1]
    token_of = jnp.zeros((expert_count * capacity,), jnp.int32).at[slot_of].set(token_ids)
    filled = (
        jnp.zeros((expert_count * capacity,), jnp.bfloat16)
        .at[slot_of]
        .set(jnp.ones_like(slot_of, dtype=jnp.bfloat16))
    )
    return (slot_of.reshape(route_block.shape), token_of, filled)


def on_device(
    queries,
    key_heads,
    value_heads,
    doc_ids,
    residual,
    ln_gain,
    expert_ids,
    expert_weight,
    w_gate,
    w_up,
    w_down,
):
    seq_len = queries.shape[1]
    kv_local = key_heads.shape[2] // HEAD_DIM
    group = queries.shape[2] // (kv_local * HEAD_DIM)
    scale = 1.0 / math.sqrt(HEAD_DIM)
    query_block = queries[0].reshape(seq_len, kv_local, group, HEAD_DIM)
    ctx_index = lax.axis_index("ctx")
    ctx_count = lax.axis_size("ctx")
    query_place = ctx_index * seq_len + jnp.arange(seq_len, dtype=jnp.int32)
    own_docs = doc_ids[0]
    key_part = lax.all_gather(key_heads, "ctx", axis=1, tiled=True)
    value_part = lax.all_gather(value_heads, "ctx", axis=1, tiled=True)
    doc_part = lax.all_gather(doc_ids, "ctx", axis=1, tiled=True)
    count = key_part.shape[1]
    key_mat = key_part[0].reshape(count, kv_local, HEAD_DIM)
    value_mat = value_part[0].reshape(count, kv_local, HEAD_DIM)
    scores = (
        jnp.einsum("tkgd,nkd->tkgn", query_block, key_mat, preferred_element_type=jnp.float32)
        * scale
    )
    key_place = jnp.arange(count, dtype=jnp.int32)
    allowed = (key_place[None, :] <= query_place[:, None]) & (
        doc_part[0][None, :] == own_docs[:, None]
    )
    allowed = allowed[:, None, None, :]
    run_max = jnp.full((seq_len, kv_local, group), -1e30, jnp.float32)
    masked = jnp.where(allowed, scores, jnp.float32(-1e30))
    new_max = jnp.maximum(run_max, jnp.max(masked, axis=-1))
    weights = jnp.where(allowed, jnp.exp(masked - new_max[..., None]), jnp.float32(0.0))
    new_total = jnp.sum(weights, axis=-1)
    added = jnp.einsum(
        "tkgn,nkd->tkgd",
        weights.astype(jnp.bfloat16),
        value_mat,
        preferred_element_type=jnp.float32,
    )
    attn_out = (added / new_total[..., None]).reshape(seq_len, -1).astype(jnp.bfloat16)
    post = residual[0].astype(jnp.float32) + attn_out.astype(jnp.float32)
    sum_post, sum_square = lax.psum((jnp.sum(post, axis=1), jnp.sum(post * post, axis=1)), "tp")
    width_full = post.shape[1] * lax.axis_size("tp")
    average = sum_post / width_full
    spread = sum_square / width_full - average * average
    normed = (
        (post - average[:, None]) * lax.rsqrt(spread + 1e-05)[:, None] * ln_gain[None, :]
    ).astype(jnp.bfloat16)
    expert_count = w_gate.shape[0] * ctx_count
    top_count = expert_ids.shape[2]
    capacity = min(seq_len, seq_len * top_count // expert_count + max(1, seq_len // 128))
    slot_of, token_of, filled = slot_table(expert_ids[0], expert_count, capacity)
    outgoing = (normed[token_of] * filled[:, None]).reshape(expert_count, capacity, -1)
    landed = lax.all_to_all(outgoing, "ctx", split_axis=0, concat_axis=0, tiled=True)
    arrived = lax.all_gather(landed, "tp", axis=2, tiled=True)
    expert_rows = arrived.reshape(-1, arrived.shape[2])
    gate_piece = lax.all_gather(w_gate, "dp", axis=1, tiled=True)
    up_piece = lax.all_gather(w_up, "dp", axis=1, tiled=True)
    gate_new = jnp.dot(expert_rows, gate_piece[0], preferred_element_type=jnp.float32)
    up_new = jnp.dot(expert_rows, up_piece[0], preferred_element_type=jnp.float32)
    hidden = (jax.nn.silu(gate_new) * up_new).astype(jnp.bfloat16)
    partial_rows = jnp.dot(
        hidden,
        lax.all_gather(w_down, "dp", axis=2, tiled=True)[0],
        preferred_element_type=jnp.float32,
    )
    summed = lax.psum_scatter(
        partial_rows.astype(jnp.bfloat16), "tp", scatter_dimension=1, tiled=True
    )
    expert_out = summed.reshape(ctx_count, capacity, -1)
    returned = lax.all_to_all(expert_out, "ctx", split_axis=0, concat_axis=0, tiled=True)
    returned = returned.reshape(expert_count * capacity, -1)
    picked = returned[slot_of].astype(jnp.float32)
    moe_out = jnp.sum(expert_weight[0][..., None] * picked, axis=1)
    return (post + moe_out).astype(jnp.bfloat16)[None]


def solution(mesh):
    placed = (
        P("dp", "ctx", "tp"),
        P("dp", "ctx", "tp"),
        P("dp", "ctx", "tp"),
        P("dp", "ctx"),
        P("dp", "ctx", "tp"),
        P("tp"),
        P("dp", "ctx", None),
        P("dp", "ctx", None),
        P("ctx", "dp", "tp"),
        P("ctx", "dp", "tp"),
        P("ctx", "tp", "dp"),
    )
    return jax.shard_map(
        on_device, mesh=mesh, in_specs=placed, out_specs=P("dp", "ctx", "tp"), check_vma=False
    )
```

profile of v0, /device:TPU:32, one launch (start us, length us, event | category | flops | bytes accessed | tf_op | source)
XLA Modules:
  0.0 583.0 jit_solution(15422538069774608477)
XLA Ops:
  6.5 0.8 copy.36
  7.6 0.6 add_select_fusion
  8.2 33.2 %all_gather.21 = s32[1,2048]{1,0:T(1,128)S(1)} all-gather(s32[1,128]{1,0:T(1,128)} %param.14), channel_id=1, replica_groups=mesh['dp'=4,'ctx'=16,'tp'=8] {'ctx'}, dimensions={1}, use_global_device_ids=true | all-gather | bytes 8704 | tf_op jit(solution)/shard_map/all_gather | solution.py:53
  41.4 33.5 %all_gather.22 = bf16[1,2048,128]{2,1,0:T(8,128)(2,1)} all-gather(bf16[1,128,128]{2,1,0:T(8,128)(2,1)} %param.12), channel_id=1, replica_groups=mesh['dp'=4,'ctx'=16,'tp'=8] {'ctx'}, dimensions={1}, use_global_device_ids=true | all-gather | bytes 557056 | tf_op jit(solution)/shard_map/all_gather | solution.py:51
  74.8 1.6 copy.29
  76.5 1.0 fusion.27
  77.5 1.7 fusion.45
  79.2 1.5 copy.31
  80.7 29.0 %all_gather.23 = bf16[1,2048,128]{1,2,0:T(8,128)(2,1)S(1)} all-gather(bf16[1,128,128]{1,2,0:T(8,128)(2,1)} %copy.31), channel_id=1, replica_groups=mesh['dp'=4,'ctx'=16,'tp'=8] {'ctx'}, dimensions={1}, use_global_device_ids=true | all-gather | bytes 557056 | tf_op jit(solution)/shard_map/all_gather | solution.py:52
  109.7 0.6 fusion.5
  110.3 1.3 fusion.24
  111.6 1.1 copy.35
  112.7 1.2 reduce-window.6
  113.9 0.2 slice_reduce_fusion
  114.3 2.6 scatter_custom_fusion
  117.0 1.0 fusion.33
  118.0 24.4 %all-reduce = (f32[128]{0:T(128)S(1)}, f32[128]{0:T(128)S(1)}) all-reduce(f32[128]{0:T(128)S(1)} %get-tuple-element.6, f32[128]{0:T(128)S(1)} %get-tuple-element.5), channel_id=1, replica_groups=mesh['dp'=4,'ctx'=16,'tp'=8] {'tp'}, use_global_device_ids=true, to_apply=%region_5.6 | all-reduce | flops 256 | bytes 2048 | tf_op jit(solution)/shard_map/psum | solution.py:79
  142.4 1.0 multiply_convert_fusion.1
  143.4 2.7 gather_fusion
  146.2 0.1 gather.9
  146.3 3.8 scatter_custom_fusion.1
  150.2 0.2 broadcast_multiply_fusion
  150.4 27.6 %all_to_all.10 = bf16[16,33,384]{2,1,0:T(8,128)(2,1)} all-to-all(bf16[16,33,384]{2,1,0:T(8,128)(2,1)S(1)} %broadcast_multiply_fusion), channel_id=1, replica_groups=mesh['dp'=4,'ctx'=16,'tp'=8] {'ctx'}, dimensions={0} | all-to-all | bytes 811008 | tf_op jit(solution)/shard_map/all_to_all | solution.py:91
  178.0 0.7 all-gather.7.cloned.1.call-update
  178.7 0.7 all-gather.9.cloned.1.call-update
  179.5 0.5 all-gather.11.cloned.1.call-update
  180.0 0.2 reduce-scatter.4.cloned.1.call-start
  180.2 75.3 %all-gather.5.cloned.1.call-done = bf16[16,33,3072]{2,1,0:T(8,128)(2,1)} async-done(((bf16[16,33,384]{2,1,0:T(8,128)(2,1)}), bf16[16,33,3072]{2,1,0:T(8,128)(2,1)}) %all-gather.5.cloned.1.call-update) | async-done | bytes 3244048 | tf_op jit(solution)/shard_map/all_gather | solution.py:92
  255.6 2.7 reshape.214
  258.2 50.6 %all-gather.7.cloned.1.call-done = bf16[1,3072,672]{1,2,0:T(8,128)(2,1)} async-done(((bf16[1,768,672]{1,2,0:T(8,128)(2,1)}), bf16[1,3072,672]{1,2,0:T(8,128)(2,1)}) %all-gather.7.cloned.1.call-update) | async-done | bytes 4128784 | tf_op jit(solution)/shard_map/all_gather | solution.py:94
  308.8 6.1 %fusion.3 = f32[528,672]{1,0:T(8,128)} fusion(bf16[528,3072]{1,0:T(8,128)(2,1)S(1)} %reshape.214, bf16[1,3072,672]{1,2,0:T(8,128)(2,1)} %all-gather.7.cloned.1.call-done), kind=kOutput, calls=%fused_computation.8 | convolution fusion | flops 2179989504 | bytes 8792064 | tf_op jit(solution)/shard_map/dot_general | solution.py:96
  315.0 50.6 %all-gather.9.cloned.1.call-done = bf16[1,3072,672]{1,2,0:T(8,128)(2,1)} async-done(((bf16[1,768,672]{1,2,0:T(8,128)(2,1)}), bf16[1,3072,672]{1,2,0:T(8,128)(2,1)}) %all-gather.9.cloned.1.call-update) | async-done | bytes 4128784 | tf_op jit(solution)/shard_map/all_gather | solution.py:95
  365.6 6.2 %multiply_convert_fusion = bf16[528,672]{1,0:T(8,128)(2,1)} fusion(f32[528,672]{1,0:T(8,128)} %fusion.3, bf16[528,3072]{1,0:T(8,128)(2,1)S(1)} %reshape.214, bf16[1,3072,672]{1,2,0:T(8,128)(2,1)} %all-gather.9.cloned.1.call-done), kind=kOutput, calls=%fused_computation.14 | convolution fusion | flops 2182118400 | bytes 9501696 | tf_op jit(solution)/shard_map/dot_general | solution.py:97
  371.7 50.4 %all-gather.11.cloned.1.call-done = bf16[1,672,3072]{2,1,0:T(8,128)(2,1)} async-done(((bf16[1,672,768]{2,1,0:T(8,128)(2,1)}), bf16[1,672,3072]{2,1,0:T(8,128)(2,1)}) %all-gather.11.cloned.1.call-update) | async-done | bytes 4128784 | tf_op jit(solution)/shard_map/all_gather | solution.py:101
  422.2 5.1 convolution_convert_fusion
  427.3 3.9 copy.42
  431.3 100.7 %reduce-scatter.4.cloned.1.call-done = bf16[384,528]{1,0:T(8,128)(2,1)} async-done(((bf16[3072,528]{1,0:T(8,128)(2,1)}), bf16[384,528]{1,0:T(8,128)(2,1)}) %reduce-scatter.4.cloned.1.call-update) | async-done | bytes 405520
  531.9 1.2 copy.43
  533.2 0.9 reshape.215
  534.1 12.6 %all-to-all-start.1 = ((bf16[16,33,384]{2,1,0:T(8,128)(2,1)}), bf16[16,33,384]{2,1,0:T(8,128)(2,1)S(1)}, u32[]{:S(2)}, u32[]{:S(2)}) async-start(bf16[16,33,384]{2,1,0:T(8,128)(2,1)} %reshape.215), calls=%async_computation.1 | async-start | bytes 983040 | tf_op jit(solution)/shard_map/all_to_all | solution.py:108
  547.0 0.1 copy.34
  547.1 0.1 copy.33
  547.2 25.7 %all-to-all-done.1 = bf16[16,33,384]{2,1,0:T(8,128)(2,1)S(1)} async-done(((bf16[16,33,384]{2,1,0:T(8,128)(2,1)}), bf16[16,33,384]{2,1,0:T(8,128)(2,1)S(1)}, u32[]{:S(2)}, u32[]{:S(2)}) %all-to-all-start.1) | async-done | bytes 405536 | tf_op jit(solution)/shard_map/all_to_all | solution.py:108
  573.0 0.1 reshape.216
  573.1 1.9 gather_fusion.1
  575.0 0.2 reshape.254
  575.2 0.5 multiply_reduce_fusion
  575.8 0.7 fusion.31
  (34 shorter events, 1.0 us)
Async XLA Ops:
  6.5 249.0 %all-gather.5.cloned.1.call-start = ((), (), s32[]{:S(2)}) async-start(), calls=%async_computation.3 | async-start | bytes 4423680 | tf_op jit(solution)/shard_map/all_gather | solution.py:92
  110.3 32.1 %copy-start.2 = (f32[384]{0:T(512)S(1)}, f32[384]{0:T(512)}, u32[]{:S(2)}) copy-start(f32[384]{0:T(512)} %param.16) | copy-start | bytes 4612
  177.9 130.9 %all-gather.7.cloned.1.call-start = ((), (), s32[]{:S(2)}) async-start(), calls=%async_computation.4 | async-start | bytes 5160960 | tf_op jit(solution)/shard_map/all_gather | solution.py:94
  178.7 186.9 %all-gather.9.cloned.1.call-start = ((), (), s32[]{:S(2)}) async-start(), calls=%async_computation.5 | async-start | bytes 5160960 | tf_op jit(solution)/shard_map/all_gather | solution.py:95
  179.4 242.7 %all-gather.11.cloned.1.call-start = ((), (), s32[]{:S(2)}) async-start(), calls=%async_computation.6 | async-start | bytes 5160960 | tf_op jit(solution)/shard_map/all_gather | solution.py:101
  180.0 351.9 %reduce-scatter.4.cloned.1.call-start = ((), (), s32[]{:S(2)}) async-start(), calls=%async_computation.7 | async-start | bytes 4423680
  431.2 115.7 %copy-start.3 = (f32[1,128,4]{1,2,0:T(4,128)S(1)}, f32[1,128,4]{1,2,0:T(4,128)}, u32[]{:S(2)}) copy-start(f32[1,128,4]{1,2,0:T(4,128)} %param.18) | copy-start | bytes 6148
  431.2 115.9 %copy-start.1 = (f32[1,128,128,3]{2,1,3,0:T(8,128)S(1)}, f32[1,128,128,3]{2,1,3,0:T(8,128)}, u32[]{:S(2)}) copy-start(f32[1,128,128,3]{2,1,3,0:T(8,128)} %fusion.24) | copy-start | bytes 589828
  534.1 38.9 %all-to-all-start.1 = ((bf16[16,33,384]{2,1,0:T(8,128)(2,1)}), bf16[16,33,384]{2,1,0:T(8,128)(2,1)S(1)}, u32[]{:S(2)}, u32[]{:S(2)}) async-start(bf16[16,33,384]{2,1,0:T(8,128)(2,1)} %reshape.215), calls=%async_computation.1 | async-start | bytes 983040 | tf_op jit(solution)/shard_map/all_to_all | solution.py:108
  547.2 28.5 %copy-start = (bf16[1,128,384]{2,1,0:T(8,128)(2,1)S(1)}, bf16[1,128,384]{2,1,0:T(8,128)(2,1)}, u32[]{:S(2)}) copy-start(bf16[1,128,384]{2,1,0:T(8,128)(2,1)} %param.15) | copy-start | bytes 294916
Sparse Core Ops, SparseCore 0:
  178.1 77.4 all-gather.4
  257.6 51.1 all-gather.6
  310.9 54.5 all-gather.8
  367.5 54.5 all-gather.10
  431.4 100.4 reduce-scatter.3
where the time goes:
time: 584 us; the launch traced here: 583 us
  waiting for transfers between devices  355 us (61%)
  blocking collectives  148 us (25%)
  local copies, waits for them, and re-layouts  26.3 us (5%)
  matrix products  20.5 us (4%)
  between operations  13.4 us (2%)
  starting transfers between devices  13 us (2%)
  other arithmetic  6.9 us (1%)
    unnamed x6, waiting for transfers between devices  103 us
    all_gather x1, waiting for transfers between devices, on_device(): arrived = lax.all_gather(landed, 'tp', axis=2, tiled=True)  75.3 us
    all_gather x1, waiting for transfers between devices, on_device(): up_piece = lax.all_gather(w_up, 'dp', axis=1, tiled=True)  50.6 us
    all_gather x1, waiting for transfers between devices, on_device(): gate_piece = lax.all_gather(w_gate, 'dp', axis=1, tiled=True)  50.6 us
    all_gather x1, waiting for transfers between devices, on_device(): lax.all_gather(w_down, 'dp', axis=2, tiled=True)[0]  50.4 us
    all_gather x1, blocking collectives, on_device(): key_part = lax.all_gather(key_heads, 'ctx', axis=1, tiled=True)  33.5 us
    all_gather x1, blocking collectives, on_device(): doc_part = lax.all_gather(doc_ids, 'ctx', axis=1, tiled=True)  33.2 us
    all_gather x1, blocking collectives, on_device(): value_part = lax.all_gather(value_heads, 'ctx', axis=1, tiled=True)  29 us
  transfers between devices with their start and end apart: 6, of which 6 were waited for; matrix products, arithmetic and copies ran while one was open for 3% of the time, Pallas kernels for 0%

commit v1 on v0

v1 whole, which is shorter than its diff:
```python
import functools
import math

import jax
import jax.numpy as jnp
from jax import lax
from jax.experimental import pallas as pl
from jax.experimental.pallas import tpu as pltpu
from jax.sharding import PartitionSpec as P

HEAD_DIM = 128
CAP = 33
REACH = 1152
BF = jnp.bfloat16
F32 = jnp.float32
VMEM = pl.BlockSpec(memory_space=pltpu.VMEM)
SMEM = pl.BlockSpec(memory_space=pltpu.SMEM)
ANY = pl.BlockSpec(memory_space=pl.ANY)
NN = (((1,), (0,)), ((), ()))
NT = (((1,), (1,)), ((), ()))
TN = (((0,), (0,)), ((), ()))


def dot(a, b, dims=NN):
    return lax.dot_general(a, b, dims, preferred_element_type=F32)


def call(body, out, specs, scratch=(), limit=32 << 20, flops=0, moved=0, name=None):
    return pl.pallas_call(
        body,
        out_shape=out,
        in_specs=specs,
        out_specs=jax.tree.map(lambda _: VMEM, out),
        scratch_shapes=list(scratch),
        compiler_params=pltpu.CompilerParams(vmem_limit_bytes=limit),
        cost_estimate=pl.CostEstimate(flops=flops, bytes_accessed=moved, transcendentals=0),
        name=name,
    )


def attend_kernel(back, v_first, place_ref, q_ref, kv_ref, rest_ref, docs_ref, res_ref, post_ref, stat_ref, scores):
    here = place_ref[0]
    rows, wide = q_ref.shape
    group = wide // HEAD_DIM
    scale = 1.0 / math.sqrt(HEAD_DIM)
    q = jnp.concatenate([q_ref[:, g * HEAD_DIM : (g + 1) * HEAD_DIM] for g in range(group)], axis=0)
    own = jnp.concatenate([docs_ref[...]] * group, axis=0)
    low = jnp.maximum(here - back, 0)
    row = lax.rem(lax.broadcasted_iota(jnp.int32, (group * rows, rows), 0), rows)
    col = lax.broadcasted_iota(jnp.int32, (group * rows, rows), 1)
    ahead = col - row
    docs_at = rows + v_first

    def first(j, top):
        s = dot(q, kv_ref[j, 0:rows, :], NT) * scale
        docs = kv_ref[j, docs_at : docs_at + 8, :][0:1, :].astype(F32)
        allowed = (docs == own) & (ahead <= (here - j) * rows)
        s = jnp.where(allowed, s, -1e30)
        scores[j - low] = s
        return jnp.maximum(top, s)

    top = lax.fori_loop(low, here + 1, first, jnp.full((group * rows, rows), -1e30, F32))
    top = jnp.max(top, axis=1, keepdims=True)

    def second(j, carry):
        total, added = carry
        s = scores[j - low]
        w = jnp.where(s > -1e29, jnp.exp(s - top), 0.0)
        values = jnp.concatenate([kv_ref[j, rows : rows + v_first, :], rest_ref[j]], axis=0)
        return total + w, added + dot(w.astype(BF), values)

    zero = jnp.zeros((group * rows, rows), F32)
    total, added = lax.fori_loop(low, here + 1, second, (zero, jnp.zeros((group * rows, HEAD_DIM), F32)))
    attn = (added / jnp.sum(total, axis=1, keepdims=True)).astype(BF).astype(F32)
    attn = jnp.concatenate([attn[g * rows : (g + 1) * rows] for g in range(group)], axis=1)
    post = res_ref[...].astype(F32) + attn
    post_ref[...] = post
    ones = jnp.ones((rows, rows), F32)
    stat_ref[0:1, :] = (jnp.sum(post, axis=1, keepdims=True) * ones).T[0:1]
    stat_ref[1:2, :] = (jnp.sum(post * post, axis=1, keepdims=True) * ones).T[0:1]
    stat_ref[2:8, :] = jnp.zeros((6, rows), F32)


def named_and_rank(ids_ref, experts):
    tokens = ids_ref.shape[1]
    expert = lax.broadcasted_iota(jnp.int32, (experts, tokens), 0)
    named = jnp.zeros((experts, tokens), F32)
    for k in range(ids_ref.shape[0]):
        named = named + jnp.where(ids_ref[k : k + 1, :] == expert, 1.0, 0.0)
    before = lax.broadcasted_iota(jnp.int32, (tokens, tokens), 0) < lax.broadcasted_iota(jnp.int32, (tokens, tokens), 1)
    rank = dot(named.astype(BF), jnp.where(before, 1.0, 0.0).astype(BF))
    return jnp.where(named > 0.5, rank, -10000.0)


def dispatch_kernel(width, post_ref, stat_ref, gain_ref, ids_ref, out_ref):
    post = post_ref[...]
    tokens, features = post.shape
    experts, rows, lanes = out_ref.shape
    stat = jnp.sum(stat_ref[...], axis=0)
    ones = jnp.ones((tokens, tokens), F32)
    average = (stat[0:1, :] * ones).T[:, 0:1] / width
    spread = (stat[1:2, :] * ones).T[:, 0:1] / width - average * average
    normed = ((post - average) * lax.rsqrt(spread + 1e-5) * gain_ref[...]).astype(BF)
    groups = features // lanes
    stacked = jnp.concatenate([normed[:, g * lanes : (g + 1) * lanes] for g in range(groups)], axis=0)
    rank = named_and_rank(ids_ref, experts).astype(jnp.int32)
    wanted = jnp.concatenate([rank + g * CAP for g in range(groups)], axis=1)
    row = lax.broadcasted_iota(jnp.int32, (rows, groups * tokens), 0)
    for e in range(experts):
        pick = jnp.where(row == wanted[e : e + 1, :], 1.0, 0.0).astype(BF)
        out_ref[e] = dot(pick, stacked).astype(BF)


def spread_kernel(in_ref, out_ref, flat):
    blocks, _, lanes = in_ref.shape
    copies, _, features = out_ref.shape
    for b in range(blocks):
        block = in_ref[b].astype(F32)
        for g in range(features // lanes):
            flat[b * CAP : (b + 1) * CAP, g * lanes : (g + 1) * lanes] = block[g * CAP : (g + 1) * CAP]
    rows = flat[...].astype(BF)
    for c in range(copies):
        out_ref[c] = rows


def expert_kernel(dp_ref, x_ref, w0, w1, w2, w3, out_ref, held, gate, up, hidden, sems):
    dp = dp_ref[0]
    order = [(p, m) for p in range(4) for m in (0, 1)] + [(p, 2) for p in range(4)]
    copies = {}
    for p, m in order:
        source = (w0, w1, w2, w3)[p]
        copies[p, m] = pltpu.make_async_copy(source.at[m], held.at[p, m], sems.at[p, m])
        copies[p, m].start()
    for p in range(4):
        j = dp ^ p
        copies[p, 0].wait()
        copies[p, 1].wait()
        x = jnp.concatenate([x_ref[2 * j], x_ref[2 * j + 1]], axis=1)
        g = dot(x, held[p, 0], NT)
        u = dot(x, held[p, 1], NT)
        if p == 0:
            gate[...] = g
            up[...] = u
        elif p < 3:
            gate[...] += g
            up[...] += u
        else:
            g = gate[...] + g
            u = up[...] + u
            hidden[...] = (g / (1.0 + jnp.exp(-g)) * u).astype(BF)
    for p in range(4):
        j = dp ^ p
        copies[p, 2].wait()
        y = dot(hidden[...], held[p, 2]).astype(BF)
        half = y.shape[1] // 2
        out_ref[2 * j] = y[:, :half]
        out_ref[2 * j + 1] = y[:, half:]


def total_kernel(in_ref, out_ref, flat):
    parts, _, features = in_ref.shape
    blocks, rows, lanes = out_ref.shape
    total = in_ref[0].astype(F32)
    for p in range(1, parts):
        total = total + in_ref[p].astype(F32)
    flat[...] = total
    groups = features // lanes
    for b in range(blocks):
        block = flat[b * CAP : (b + 1) * CAP, :]
        runs = [block[:, g * lanes : (g + 1) * lanes] for g in range(groups)]
        runs.append(jnp.zeros((rows - groups * CAP, lanes), F32))
        out_ref[b] = jnp.concatenate(runs, axis=0).astype(BF)


def combine_kernel(post_ref, ids_ref, weight_ref, back_ref, out_ref):
    tokens, features = post_ref.shape
    experts, rows, lanes = back_ref.shape
    groups = features // lanes
    rank = named_and_rank(ids_ref, experts).astype(jnp.int32)
    expert = lax.broadcasted_iota(jnp.int32, (experts, tokens), 0)
    weight = jnp.zeros((experts, tokens), F32)
    for k in range(ids_ref.shape[0]):
        weight = weight + jnp.where(ids_ref[k : k + 1, :] == expert, weight_ref[k : k + 1, :], 0.0)
    wide_rank = jnp.concatenate([rank + g * CAP for g in range(groups)], axis=1)
    wide_weight = jnp.concatenate([weight] * groups, axis=1)
    row = lax.broadcasted_iota(jnp.int32, (rows, groups * tokens), 0)
    moe = jnp.zeros((groups * tokens, lanes), F32)
    for e in range(experts):
        pick = jnp.where(row == wide_rank[e : e + 1, :], wide_weight[e : e + 1, :], 0.0)
        upper = pick.astype(BF)
        lower = (pick - upper.astype(F32)).astype(BF)
        moe = moe + dot(upper, back_ref[e], TN) + dot(lower, back_ref[e], TN)
    moe = jnp.concatenate([moe[g * tokens : (g + 1) * tokens] for g in range(groups)], axis=1)
    out_ref[...] = (post_ref[...] + moe).astype(BF)


def all_to_all(x, axis):
    return lax.all_to_all(x, axis, split_axis=0, concat_axis=0, tiled=True)


def on_device(
    queries,
    key_heads,
    value_heads,
    doc_ids,
    residual,
    ln_gain,
    expert_ids,
    expert_weight,
    w_gate,
    w_up,
    w_down,
):
    rows = queries.shape[1]
    features = residual.shape[2]
    ctx_count = lax.axis_size("ctx")
    tp_count = lax.axis_size("tp")
    dp_index = lax.axis_index("dp").reshape(1)
    ctx_index = lax.axis_index("ctx").reshape(1)
    ids = expert_ids[0].T
    weight = expert_weight[0].T
    hidden_units = w_down.shape[1]

    w_own = jnp.stack([w_gate[0].T, w_up[0].T, w_down[0]])
    other_chip = [(i, i ^ 2) for i in range(4)]
    other_core = [(i, i ^ 1) for i in range(4)]
    w_chip = lax.ppermute(w_own, "dp", other_chip)
    w_core = lax.ppermute(w_own, "dp", other_core)

    v_first = rows - 16
    docs_row = jnp.broadcast_to(doc_ids.astype(BF), (8, rows))
    packed = jnp.concatenate([key_heads[0], value_heads[0, :v_first], docs_row], axis=0)
    rest = all_to_all(jnp.broadcast_to(value_heads[:, v_first:], (ctx_count, rows - v_first, HEAD_DIM)), "ctx")
    kv = lax.all_gather(packed, "ctx", axis=0)
    back = -(-(REACH - 1) // rows)
    group = queries.shape[2] // HEAD_DIM
    post, stat = call(
        functools.partial(attend_kernel, back, v_first),
        (jax.ShapeDtypeStruct((rows, features), F32), jax.ShapeDtypeStruct((8, rows), F32)),
        [SMEM] + [VMEM] * 5,
        [pltpu.VMEM((back + 1, group * rows, rows), F32)],
        name="attend",
    )(ctx_index, queries[0], kv, rest, doc_ids[0].astype(F32).reshape(rows, 1), residual[0])

    stats = all_to_all(jnp.broadcast_to(stat[None], (tp_count,) + stat.shape), "tp")
    block = -(-(features // 128 * CAP) // 8) * 8
    outgoing = call(
        functools.partial(dispatch_kernel, features * tp_count),
        jax.ShapeDtypeStruct((ctx_count, block, 128), BF),
        [VMEM] * 4,
        name="dispatch",
    )(post, stats, ln_gain.reshape(1, features), ids)
    landed = all_to_all(outgoing, "ctx")
    landed, w_chip = lax.optimization_barrier((landed, w_chip))
    w_both = lax.ppermute(w_chip, "dp", other_core)
    total_rows = ctx_count * CAP
    copies = call(
        spread_kernel,
        jax.ShapeDtypeStruct((tp_count, total_rows, features), BF),
        [VMEM],
        [pltpu.VMEM((total_rows, features), F32)],
        name="spread",
    )(landed)
    arrived = all_to_all(copies, "tp")
    partial = call(
        expert_kernel,
        jax.ShapeDtypeStruct((tp_count, total_rows, features), BF),
        [SMEM, VMEM, ANY, ANY, ANY, ANY],
        [
            pltpu.VMEM((4, 3, hidden_units, w_down.shape[2]), BF),
            pltpu.VMEM((total_rows, hidden_units), F32),
            pltpu.VMEM((total_rows, hidden_units), F32),
            pltpu.VMEM((total_rows, hidden_units), BF),
            pltpu.SemaphoreType.DMA((4, 3)),
        ],
        limit=48 << 20,
        flops=6 * total_rows * hidden_units * features * tp_count,
        moved=24 << 20,
        name="expert",
    )(dp_index, arrived, w_own, w_core, w_chip, w_both)
    groups = all_to_all(partial, "tp")
    expert_out = call(
        total_kernel,
        jax.ShapeDtypeStruct((ctx_count, block, 128), BF),
        [VMEM],
        [pltpu.VMEM((total_rows, features), F32)],
        name="total",
    )(groups)
    returned = all_to_all(expert_out, "ctx")
    mixed = call(
        combine_kernel,
        jax.ShapeDtypeStruct((rows, features), BF),
        [VMEM] * 4,
        name="combine",
    )(post, ids, weight, returned)
    return mixed[None]


def solution(mesh):
    placed = (
        P("dp", "ctx", "tp"),
        P("dp", "ctx", "tp"),
        P("dp", "ctx", "tp"),
        P("dp", "ctx"),
        P("dp", "ctx", "tp"),
        P("tp"),
        P("dp", "ctx", None),
        P("dp", "ctx", None),
        P("ctx", "dp", "tp"),
        P("ctx", "dp", "tp"),
        P("ctx", "tp", "dp"),
    )
    return jax.shard_map(
        on_device, mesh=mesh, in_specs=placed, out_specs=P("dp", "ctx", "tp"), check_vma=False
    )
```

time: 584 us -> 263 us (0.45)
  the two profiles are of different devices: /device:TPU:32 before, /device:TPU:64 now
where the time goes in v1:
time: 263 us; the launch traced here: 262 us
  blocking collectives  110 us (42%)
  waiting for transfers between devices  75.7 us (29%)
  starting transfers between devices  47.8 us (18%)
  Pallas kernels  23.3 us (9%)
  other arithmetic  3.98 us (2%)
    all_to_all x4, waiting for transfers between devices, all_to_all(): return lax.all_to_all(x, axis, split_axis=0, concat_axis=0, tiled=True)  75.7 us
    all_to_all x2, blocking collectives, all_to_all(): return lax.all_to_all(x, axis, split_axis=0, concat_axis=0, tiled=True)  75.6 us
    all_to_all x4, starting transfers between devices, all_to_all(): return lax.all_to_all(x, axis, split_axis=0, concat_axis=0, tiled=True)  40.6 us
    all_gather x1, blocking collectives, on_device(): kv = lax.all_gather(packed, 'ctx', axis=0)  33.9 us
    pallas_call x1, Pallas kernels, on_device(): call(expert_kernel, jax.ShapeDtypeStruct((tp_count, total_rows, features)...  15.2 us
  transfers between devices with their start and end apart: 7, of which 3 were waited for; matrix products, arithmetic and copies ran while one was open for 1% of the time, Pallas kernels for 2%

profile of v1, /device:TPU:64, one launch (start us, length us, event | category | flops | bytes accessed | tf_op | source)
XLA Modules:
  0.0 261.9 jit_solution(2252626324662525394)
XLA Ops:
  0.0 0.0 copy-start.4
  0.0 0.0 copy-start.7
  0.0 0.0 copy-start.5
  0.0 0.0 copy-start
  0.0 0.0 copy-start.1
  0.0 0.0 copy-start.6
  0.0 0.0 copy-start.2
  0.0 4.0 %pad_maximum_fusion.w0 = bf16[3,672,768]{2,1,0:T(8,128)(2,1)} fusion(bf16[1,672,768]{2,1,0:T(8,128)(2,1)} %param.21, bf16[1,672,768]{2,1,0:T(8,128)(2,1)} %bitcast.37, bf16[1,672,768]{2,1,0:T(8,128)(2,1)} %bitcast.38), kind=kLoop, calls=%fused_computation | loop fusion | flops 3096576 | bytes 6193152 | tf_op jit(solution)/shard_map/stack | solution.py:224
  4.0 3.4 %collective-permute-start = (bf16[3,672,768]{2,1,0:T(8,128)(2,1)}, bf16[3,672,768]{2,1,0:T(8,128)(2,1)}, u32[]{:S(2)}, u32[]{:S(2)}) collective-permute-start(bf16[3,672,768]{2,1,0:T(8,128)(2,1)} %pad_maximum_fusion.w0), channel_id=1, source_target_pairs={{0,256},{128,384},{256,0},{384,128},{1,257},{129,385},{257,1},{385... | collective-permute-start | bytes 9289736 | tf_op jit(solution)/shard_map/ppermute | solution.py:227
  7.4 0.0 copy-done.4
  7.4 0.6 broadcast_in_dim.26
  8.1 14.8 %all-to-all-start = ((bf16[16,16,128]{2,1,0:T(8,128)(2,1)}), bf16[16,16,128]{2,1,0:T(8,128)(2,1)S(1)}, u32[]{:S(2)}, u32[]{:S(2)}) async-start(bf16[16,16,128]{2,1,0:T(8,128)(2,1)} %broadcast_in_dim.26), calls=%async_computation | async-start | bytes 131072 | tf_op jit(solution)/shard_map/all_to_all | solution.py:198
  22.8 0.0 copy-done.7
  22.8 0.1 copy.12.docs_ref
  23.0 0.0 copy-done.5
  23.0 33.9 %all-gather = bf16[3968,128]{1,0:T(8,128)(2,1)S(1)} all-gather(bf16[248,128]{1,0:T(8,128)(2,1)S(1)} %pad_maximum_fusion.1), channel_id=2, replica_groups=mesh['dp'=4,'ctx'=16,'tp'=8] {'ctx'}, dimensions={0}, use_global_device_ids=true | all-gather | bytes 1079296 | tf_op jit(solution)/shard_map/all_gather | solution.py:234
  56.9 0.0 all-to-all-done.rest_ref
  56.9 0.0 copy-done
  56.9 0.0 copy-done.1
  56.9 1.7 attend.1
  58.6 0.6 broadcast_in_dim.27
  59.3 6.6 %all-to-all-start.1 = ((f32[8,8,128]{2,1,0:T(8,128)}), f32[8,8,128]{2,1,0:T(8,128)S(1)}, u32[]{:S(2)}, u32[]{:S(2)}) async-start(f32[8,8,128]{2,1,0:T(8,128)} %broadcast_in_dim.27), calls=%async_computation.1 | async-start | bytes 65536 | tf_op jit(solution)/shard_map/all_to_all | solution.py:198
  65.9 0.0 copy-done.6
  65.9 14.1 %all-to-all-done.1.stat_ref = f32[8,8,128]{2,1,0:T(8,128)S(1)} async-done(((f32[8,8,128]{2,1,0:T(8,128)}), f32[8,8,128]{2,1,0:T(8,128)S(1)}, u32[]{:S(2)}, u32[]{:S(2)}) %all-to-all-start.1) | async-done | bytes 32800 | tf_op jit(solution)/shard_map/all_to_all | solution.py:198
  80.0 0.0 copy-done.2
  80.0 1.6 dispatch.1
  81.6 14.8 %all-to-all-start.2 = ((bf16[16,104,128]{2,1,0:T(8,128)(2,1)}), bf16[16,104,128]{2,1,0:T(8,128)(2,1)S(1)}, u32[]{:S(2)}, u32[]{:S(2)}) async-start(bf16[16,104,128]{2,1,0:T(8,128)(2,1)} %dispatch.1), calls=%async_computation.2 | async-start | bytes 851968 | tf_op jit(solution)/shard_map/all_to_all | solution.py:198
  96.3 1.9 collective-permute-start.1
  98.2 22.0 %all-to-all-done.2.in_ref = bf16[16,104,128]{2,1,0:T(8,128)(2,1)S(1)} async-done(((bf16[16,104,128]{2,1,0:T(8,128)(2,1)}), bf16[16,104,128]{2,1,0:T(8,128)(2,1)S(1)}, u32[]{:S(2)}, u32[]{:S(2)}) %all-to-all-start.2) | async-done | bytes 426016 | tf_op jit(solution)/shard_map/all_to_all | solution.py:198
  120.2 0.0 collective-permute-done.w2
  120.2 1.9 collective-permute-start.2
  122.1 2.1 spread.1
  124.2 4.5 %all-to-all-start.3 = ((bf16[8,528,384]{2,1,0:T(8,128)(2,1)}), bf16[8,528,384]{2,1,0:T(8,128)(2,1)}, u32[]{:S(2)}, u32[]{:S(2)}) async-start(bf16[8,528,384]{2,1,0:T(8,128)(2,1)} %spread.1), calls=%async_computation.3 | async-start | bytes 6488064 | tf_op jit(solution)/shard_map/all_to_all | solution.py:198
  128.7 0.0 collective-permute-done.1.w1
  128.7 39.6 %all-to-all-done.3.x_ref = bf16[8,528,384]{2,1,0:T(8,128)(2,1)} async-done(((bf16[8,528,384]{2,1,0:T(8,128)(2,1)}), bf16[8,528,384]{2,1,0:T(8,128)(2,1)}, u32[]{:S(2)}, u32[]{:S(2)}) %all-to-all-start.3) | async-done | bytes 3244064 | tf_op jit(solution)/shard_map/all_to_all | solution.py:198
  168.3 0.0 collective-permute-done.2.w3
  168.3 15.2 %expert.1 = bf16[8,528,384]{2,1,0:T(8,128)(2,1)} custom-call(s32[1]{0:T(128)} %bitcast.13.dp_ref, bf16[8,528,384]{2,1,0:T(8,128)(2,1)} %all-to-all-done.3.x_ref, bf16[3,672,768]{2,1,0:T(8,128)(2,1)} %pad_maximum_fusion.w0, bf16[3,672,768]{2,1,0:T(8,128)(2,1)} %collective-permute-done.1.w1, bf16[3,672,768]{2,1,0:T(8,128)(2,1)} %collective-permute-done.w2, ...), custom_call_target="tpu_custom_call" | custom-call | flops 6539968512 | bytes 25165824 | tf_op jit(solution)/shard_map/expert/pallas_call | solution.py:265
  183.5 45.8 %all_to_all.30.in_ref = bf16[8,528,384]{2,1,0:T(8,128)(2,1)S(1)} all-to-all(bf16[8,528,384]{2,1,0:T(8,128)(2,1)} %expert.1), channel_id=1, replica_groups=mesh['dp'=4,'ctx'=16,'tp'=8] {'tp'}, dimensions={0} | all-to-all | bytes 6488064 | tf_op jit(solution)/shard_map/all_to_all | solution.py:198
  229.3 0.0 copy-start.3
  229.3 0.8 total.1
  230.1 29.9 %all_to_all.31.back_ref = bf16[16,104,128]{2,1,0:T(8,128)(2,1)S(1)} all-to-all(bf16[16,104,128]{2,1,0:T(8,128)(2,1)S(1)} %total.1), channel_id=1, replica_groups=mesh['dp'=4,'ctx'=16,'tp'=8] {'ctx'}, dimensions={0} | all-to-all | bytes 851968 | tf_op jit(solution)/shard_map/all_to_all | solution.py:198
  260.0 0.0 copy-done.3
  260.0 1.9 combine.1
  (6 shorter events, 0.0 us)
Async XLA Ops:
  0.0 7.4 %copy-start.4 = (bf16[1,128,128]{2,1,0:T(8,128)(2,1)S(1)}, bf16[1,128,128]{2,1,0:T(8,128)(2,1)}, u32[]{:S(2)}) copy-start(bf16[1,128,128]{2,1,0:T(8,128)(2,1)} %param.13) | copy-start | bytes 98308
  0.0 22.8 %copy-start.7 = (s32[1,128]{1,0:T(1,128)S(1)}, s32[1,128]{1,0:T(1,128)}, u32[]{:S(2)}) copy-start(s32[1,128]{1,0:T(1,128)} %param.14) | copy-start | bytes 1540
  0.0 23.0 %copy-start.5 = (bf16[1,128,128]{2,1,0:T(8,128)(2,1)S(1)}, bf16[1,128,128]{2,1,0:T(8,128)(2,1)}, u32[]{:S(2)}) copy-start(bf16[1,128,128]{2,1,0:T(8,128)(2,1)} %param.12) | copy-start | bytes 98308
  0.0 56.9 %copy-start = (bf16[1,128,384]{2,1,0:T(8,128)(2,1)S(1)}, bf16[1,128,384]{2,1,0:T(8,128)(2,1)}, u32[]{:S(2)}) copy-start(bf16[1,128,384]{2,1,0:T(8,128)(2,1)} %param.11) | copy-start | bytes 294916
  0.0 56.9 %copy-start.1 = (bf16[1,128,384]{2,1,0:T(8,128)(2,1)S(1)}, bf16[1,128,384]{2,1,0:T(8,128)(2,1)}, u32[]{:S(2)}) copy-start(bf16[1,128,384]{2,1,0:T(8,128)(2,1)} %param.15) | copy-start | bytes 294916
  0.0 65.9 %copy-start.6 = (f32[384]{0:T(512)S(1)}, f32[384]{0:T(512)}, u32[]{:S(2)}) copy-start(f32[384]{0:T(512)} %param.16) | copy-start | bytes 4612
  0.0 79.9 %copy-start.2 = (s32[1,128,4]{1,2,0:T(4,128)S(1)}, s32[1,128,4]{1,2,0:T(4,128)}, u32[]{:S(2)}) copy-start(s32[1,128,4]{1,2,0:T(4,128)} %param.17) | copy-start | bytes 6148
  4.0 116.2 %collective-permute-start = (bf16[3,672,768]{2,1,0:T(8,128)(2,1)}, bf16[3,672,768]{2,1,0:T(8,128)(2,1)}, u32[]{:S(2)}, u32[]{:S(2)}) collective-permute-start(bf16[3,672,768]{2,1,0:T(8,128)(2,1)} %pad_maximum_fusion.w0), channel_id=1, source_target_pairs={{0,256},{128,384},{256,0},{384,128},{1,257},{129,385},{257,1},{385... | collective-permute-start | bytes 9289736 | tf_op jit(solution)/shard_map/ppermute | solution.py:227
  8.1 48.8 %all-to-all-start = ((bf16[16,16,128]{2,1,0:T(8,128)(2,1)}), bf16[16,16,128]{2,1,0:T(8,128)(2,1)S(1)}, u32[]{:S(2)}, u32[]{:S(2)}) async-start(bf16[16,16,128]{2,1,0:T(8,128)(2,1)} %broadcast_in_dim.26), calls=%async_computation | async-start | bytes 131072 | tf_op jit(solution)/shard_map/all_to_all | solution.py:198
  59.3 20.7 %all-to-all-start.1 = ((f32[8,8,128]{2,1,0:T(8,128)}), f32[8,8,128]{2,1,0:T(8,128)S(1)}, u32[]{:S(2)}, u32[]{:S(2)}) async-start(f32[8,8,128]{2,1,0:T(8,128)} %broadcast_in_dim.27), calls=%async_computation.1 | async-start | bytes 65536 | tf_op jit(solution)/shard_map/all_to_all | solution.py:198
  81.6 38.6 %all-to-all-start.2 = ((bf16[16,104,128]{2,1,0:T(8,128)(2,1)}), bf16[16,104,128]{2,1,0:T(8,128)(2,1)S(1)}, u32[]{:S(2)}, u32[]{:S(2)}) async-start(bf16[16,104,128]{2,1,0:T(8,128)(2,1)} %dispatch.1), calls=%async_computation.2 | async-start | bytes 851968 | tf_op jit(solution)/shard_map/all_to_all | solution.py:198
  96.3 32.3 %collective-permute-start.1 = (bf16[3,672,768]{2,1,0:T(8,128)(2,1)}, bf16[3,672,768]{2,1,0:T(8,128)(2,1)}, u32[]{:S(2)}, u32[]{:S(2)}) collective-permute-start(bf16[3,672,768]{2,1,0:T(8,128)(2,1)} %pad_maximum_fusion.w0), channel_id=1, source_target_pairs={{0,128},{128,0},{256,384},{384,256},{1,129},{129,1},{257,385},{385... | collective-permute-start | bytes 9289736 | tf_op jit(solution)/shard_map/ppermute | solution.py:228
  120.2 48.1 %collective-permute-start.2 = (bf16[3,672,768]{2,1,0:T(8,128)(2,1)}, bf16[3,672,768]{2,1,0:T(8,128)(2,1)}, u32[]{:S(2)}, u32[]{:S(2)}) collective-permute-start(bf16[3,672,768]{2,1,0:T(8,128)(2,1)} %collective-permute-done.w2), channel_id=1, source_target_pairs={{0,128},{128,0},{256,384},{384,256},{1,129},{129,1},{257,385},{385... | collective-permute-start | bytes 9289736 | tf_op jit(solution)/shard_map/ppermute | solution.py:255
  124.2 44.1 %all-to-all-start.3 = ((bf16[8,528,384]{2,1,0:T(8,128)(2,1)}), bf16[8,528,384]{2,1,0:T(8,128)(2,1)}, u32[]{:S(2)}, u32[]{:S(2)}) async-start(bf16[8,528,384]{2,1,0:T(8,128)(2,1)} %spread.1), calls=%async_computation.3 | async-start | bytes 6488064 | tf_op jit(solution)/shard_map/all_to_all | solution.py:198
  229.3 30.7 %copy-start.3 = (f32[1,128,4]{1,2,0:T(4,128)S(1)}, f32[1,128,4]{1,2,0:T(4,128)}, u32[]{:S(2)}) copy-start(f32[1,128,4]{1,2,0:T(4,128)} %param.18) | copy-start | bytes 6148

commit v2 on v1

v2 whole, which is shorter than its diff:
```python
import functools
import math

import jax
import jax.numpy as jnp
from jax import lax
from jax.experimental import pallas as pl
from jax.experimental.pallas import tpu as pltpu
from jax.sharding import PartitionSpec as P

HEAD_DIM = 128
CAP = 33
FULL = 58 << 20
REACH = 1152
BF = jnp.bfloat16
F32 = jnp.float32
VMEM = pl.BlockSpec(memory_space=pltpu.VMEM)
SMEM = pl.BlockSpec(memory_space=pltpu.SMEM)
ANY = pl.BlockSpec(memory_space=pl.ANY)
NN = (((1,), (0,)), ((), ()))
NT = (((1,), (1,)), ((), ()))
TN = (((0,), (0,)), ((), ()))


def dot(a, b, dims=NN):
    return lax.dot_general(a, b, dims, preferred_element_type=F32)


def call(body, out, specs, scratch=(), out_spec=VMEM, limit=32 << 20, flops=0, moved=0, name=None):
    return pl.pallas_call(
        body,
        out_shape=out,
        in_specs=specs,
        out_specs=jax.tree.map(lambda _: out_spec, out),
        scratch_shapes=list(scratch),
        compiler_params=pltpu.CompilerParams(vmem_limit_bytes=limit),
        cost_estimate=pl.CostEstimate(flops=flops, bytes_accessed=moved, transcendentals=0),
        name=name,
    )


def terms(x, count):
    out = []
    for _ in range(count):
        part = x.astype(BF).astype(F32)
        out.append(part)
        x = x - part
    return out


def stack_kernel(*refs):
    *sources, out_ref, held, arrive, leave = refs
    into = [pltpu.make_async_copy(source, held.at[i], arrive.at[i]) for i, source in enumerate(sources)]
    away = [pltpu.make_async_copy(held.at[i], out_ref.at[i], leave.at[i]) for i in range(len(sources))]
    for copy in into:
        copy.start()
    for first, then in zip(into, away):
        first.wait()
        then.start()
    for copy in away:
        copy.wait()


def named_and_rank(ids_ref, experts):
    tokens = ids_ref.shape[1]
    expert = lax.broadcasted_iota(jnp.int32, (experts, tokens), 0)
    named = jnp.zeros((experts, tokens), F32)
    for k in range(ids_ref.shape[0]):
        named = named + jnp.where(ids_ref[k : k + 1, :] == expert, 1.0, 0.0)
    before = lax.broadcasted_iota(jnp.int32, (tokens, tokens), 0) < lax.broadcasted_iota(jnp.int32, (tokens, tokens), 1)
    rank = dot(named.astype(BF), jnp.where(before, 1.0, 0.0).astype(BF))
    return jnp.where(named > 0.5, rank, -10000.0)


def attend_kernel(
    back, v_first, place_ref, q_ref, kv_ref, rest_ref, docs_ref, res_ref, ids_ref, post_ref, out_ref, scores
):
    here = place_ref[0]
    rows, wide = q_ref.shape
    group = wide // HEAD_DIM
    scale = 1.0 / math.sqrt(HEAD_DIM)
    q = jnp.concatenate([q_ref[:, g * HEAD_DIM : (g + 1) * HEAD_DIM] for g in range(group)], axis=0)
    own = jnp.concatenate([docs_ref[...]] * group, axis=0)
    low = jnp.maximum(here - back, 0)
    row = lax.rem(lax.broadcasted_iota(jnp.int32, (group * rows, rows), 0), rows)
    col = lax.broadcasted_iota(jnp.int32, (group * rows, rows), 1)
    ahead = col - row
    docs_at = rows + v_first

    def first(j, top):
        s = dot(q, kv_ref[j, 0:rows, :], NT) * scale
        docs = kv_ref[j, docs_at : docs_at + 8, :][0:1, :].astype(F32)
        allowed = (docs == own) & (ahead <= (here - j) * rows)
        s = jnp.where(allowed, s, -1e30)
        scores[j - low] = s
        return jnp.maximum(top, s)

    top = lax.fori_loop(low, here + 1, first, jnp.full((group * rows, rows), -1e30, F32))
    top = jnp.max(top, axis=1, keepdims=True)

    def second(j, carry):
        total, added = carry
        s = scores[j - low]
        w = jnp.where(s > -1e29, jnp.exp(s - top), 0.0)
        values = jnp.concatenate([kv_ref[j, rows : rows + v_first, :], rest_ref[j]], axis=0)
        return total + w, added + dot(w.astype(BF), values)

    zero = jnp.zeros((group * rows, rows), F32)
    total, added = lax.fori_loop(low, here + 1, second, (zero, jnp.zeros((group * rows, HEAD_DIM), F32)))
    attn = (added / jnp.sum(total, axis=1, keepdims=True)).astype(BF).astype(F32)
    attn = jnp.concatenate([attn[g * rows : (g + 1) * rows] for g in range(group)], axis=1)
    post = res_ref[...].astype(F32) + attn
    post_ref[...] = post

    experts, block, lanes = out_ref.shape
    groups = wide // lanes
    mean = jnp.mean(post, axis=1, keepdims=True)
    centred = post - mean
    square = jnp.sum(centred * centred, axis=1, keepdims=True)
    centred = centred.astype(BF)
    ones = jnp.ones((rows, rows), F32)
    parts = terms((mean * ones).T[0:1], 3) + terms((square * ones).T[0:1], 2)
    parts = jnp.concatenate(parts + [jnp.zeros((3, rows), F32)], axis=0).astype(BF)
    stacked = jnp.concatenate([centred[:, g * lanes : (g + 1) * lanes] for g in range(groups)], axis=0)
    rank = named_and_rank(ids_ref, experts).astype(jnp.int32)
    wanted = jnp.concatenate([rank + g * CAP for g in range(groups)], axis=1)
    place = lax.broadcasted_iota(jnp.int32, (block, groups * rows), 0)
    slot = lax.broadcasted_iota(jnp.int32, (lanes, rows), 0)
    for e in range(experts):
        pick = jnp.where(place == wanted[e : e + 1, :], 1.0, 0.0).astype(BF)
        data = dot(pick, stacked)
        pick = jnp.where(slot == rank[e : e + 1, :], 1.0, 0.0).astype(BF)
        stats = dot(parts, pick, NT)
        out_ref[e] = jnp.concatenate([data[: groups * CAP], stats[: block - groups * CAP]], axis=0).astype(BF)


def spread_kernel(in_ref, gain_ref, out_ref, flat):
    blocks, block, lanes = in_ref.shape
    copies, _, features = out_ref.shape
    groups = features // lanes
    half = blocks // 2
    stats = []
    for b in range(blocks):
        x = in_ref[b].astype(F32)
        for g in range(groups):
            flat[b * CAP : (b + 1) * CAP, g * lanes : (g + 1) * lanes] = x[g * CAP : (g + 1) * CAP]
        stats.append(jnp.concatenate([x[groups * CAP :], jnp.zeros((8 - block + groups * CAP, lanes), F32)], axis=0))
    at = lax.broadcasted_iota(jnp.int32, (half * lanes, features), 0)
    lane = lax.broadcasted_iota(jnp.int32, (half * lanes, features), 1)
    slot = lax.rem(at, lanes)
    put = jnp.where((lane == lax.div(at, lanes) * CAP + slot) & (slot < CAP), 1.0, 0.0).astype(BF)
    top = blocks * CAP
    for h in range(2):
        mine = jnp.concatenate(stats[h * half : (h + 1) * half], axis=1).astype(BF)
        flat[top + 5 * h : top + 5 * h + 5, :] = dot(mine, put)[0:5]
    flat[top + 10 : top + 16, :] = jnp.concatenate(
        terms(gain_ref[...], 3) + [jnp.zeros((3, features), F32)], axis=0
    )
    result = flat[...].astype(BF)
    for c in range(copies):
        out_ref[c] = result


def expert_kernel(
    dp_ref, x_ref, g0, g1, g2, g3, d0, d1, d2, d3, out_ref, x_in, tails, held, gate, up, hidden, column, y_out, sems, more
):
    dp = dp_ref[0]
    parts, total, features = x_ref.shape
    rows = total - 16
    half = rows // 2
    arriving = {("tails",): pltpu.make_async_copy(x_ref.at[:, pl.ds(rows, 16), :], tails, more.at[8])}
    for p in range(4):
        for i in range(2):
            source = x_ref.at[2 * (dp ^ p) + i, pl.ds(0, rows), :]
            arriving["x", p, i] = pltpu.make_async_copy(source, x_in.at[2 * p + i], more.at[2 * p + i])
        for m in range(3):
            source = (d0, d1, d2, d3)[p] if m == 2 else (g0, g1, g2, g3)[p].at[m]
            arriving[p, m] = pltpu.make_async_copy(source, held.at[p, m], sems.at[p, m])

    def begin(*keys):
        for key in keys:
            arriving[key].start()

    def piece(p):
        return ("x", p, 0), ("x", p, 1), (p, 0), (p, 1)

    begin(("tails",), *piece(0))
    arriving["tails",].wait()
    begin(*piece(1))
    means, squares = [], []
    for q in range(parts):
        tail = tails[q].astype(F32)
        means.append([tail[5 * h : 5 * h + 1] + tail[5 * h + 1 : 5 * h + 2] + tail[5 * h + 2 : 5 * h + 3] for h in (0, 1)])
        squares.append([tail[5 * h + 3 : 5 * h + 4] + tail[5 * h + 4 : 5 * h + 5] for h in (0, 1)])
    for h in (0, 1):
        average = sum(m[h] for m in means) / parts
        shifts = [m[h] - average for m in means]
        spread = (sum(s[h] for s in squares) + features * sum(s * s for s in shifts)) / (parts * features)
        block = jnp.concatenate(shifts + [lax.rsqrt(spread + 1e-5), jnp.zeros((128 - parts - 1, features), F32)], axis=0)
        column[h * half : (h + 1) * half, :] = block.T[0:half]

    def normed(p, i):
        q = 2 * (dp ^ p) + i
        tail = tails[q].astype(F32)
        gain = tail[10:11] + tail[11:12] + tail[12:13]
        at = lax.broadcasted_iota(jnp.int32, (rows, 128), 1)
        shift = jnp.sum(jnp.where(at == q, column[...], 0.0), axis=1, keepdims=True)
        scale = column[:, parts : parts + 1]
        arriving["x", p, i].wait()
        return ((x_in[2 * p + i].astype(F32) + shift) * scale * gain).astype(BF)

    for p in range(4):
        x = jnp.concatenate([normed(p, 0), normed(p, 1)], axis=1)
        arriving[p, 0].wait()
        arriving[p, 1].wait()
        if p < 2:
            begin(*piece(p + 2))
        else:
            begin((2 * p - 4, 2), (2 * p - 3, 2))
        g = dot(x, held[p, 0], NT)
        u = dot(x, held[p, 1], NT)
        if p == 0:
            gate[...] = g
            up[...] = u
        elif p < 3:
            gate[...] += g
            up[...] += u
        else:
            g = gate[...] + g
            u = up[...] + u
            hidden[...] = (g / (1.0 + jnp.exp(-g)) * u).astype(BF)
    leaving = []
    for p in range(4):
        j = dp ^ p
        arriving[p, 2].wait()
        y = dot(hidden[...], held[p, 2]).astype(BF)
        for i in range(2):
            y_out[2 * p + i] = y[:, i * features : (i + 1) * features]
            leaving.append(pltpu.make_async_copy(y_out.at[2 * p + i], out_ref.at[2 * j + i], more.at[9 + 2 * p + i]))
            leaving[-1].start()
    for copy in leaving:
        copy.wait()


def total_kernel(in_ref, out_ref, flat):
    parts, _, features = in_ref.shape
    blocks, rows, lanes = out_ref.shape
    total = in_ref[0].astype(F32)
    for p in range(1, parts):
        total = total + in_ref[p].astype(F32)
    flat[...] = total
    groups = features // lanes
    for b in range(blocks):
        block = flat[b * CAP : (b + 1) * CAP, :]
        runs = [block[:, g * lanes : (g + 1) * lanes] for g in range(groups)]
        runs.append(jnp.zeros((rows - groups * CAP, lanes), F32))
        out_ref[b] = jnp.concatenate(runs, axis=0).astype(BF)


def weigh_kernel(term, ids_ref, weight_ref, out_ref):
    experts, rows, wide = out_ref.shape
    tokens = ids_ref.shape[1]
    groups = wide // tokens
    rank = named_and_rank(ids_ref, experts).astype(jnp.int32)
    expert = lax.broadcasted_iota(jnp.int32, (experts, tokens), 0)
    weight = jnp.zeros((experts, tokens), F32)
    for k in range(ids_ref.shape[0]):
        weight = weight + jnp.where(ids_ref[k : k + 1, :] == expert, weight_ref[k : k + 1, :], 0.0)
    weight = terms(weight, 2)[term]
    wide_rank = jnp.concatenate([rank + g * CAP for g in range(groups)], axis=1)
    wide_weight = jnp.concatenate([weight] * groups, axis=1)
    row = lax.broadcasted_iota(jnp.int32, (rows, wide), 0)
    for e in range(experts):
        out_ref[e] = jnp.where(row == wide_rank[e : e + 1, :], wide_weight[e : e + 1, :], 0.0).astype(BF)


def combine_kernel(post_ref, upper_ref, lower_ref, back_ref, out_ref):
    tokens, features = post_ref.shape
    experts, rows, lanes = back_ref.shape
    groups = features // lanes
    moe = jnp.zeros((groups * tokens, lanes), F32)
    for e in range(experts):
        moe = moe + dot(upper_ref[e], back_ref[e], TN) + dot(lower_ref[e], back_ref[e], TN)
    moe = jnp.concatenate([moe[g * tokens : (g + 1) * tokens] for g in range(groups)], axis=1)
    out_ref[...] = (post_ref[...] + moe).astype(BF)


def all_to_all(x, axis):
    return lax.all_to_all(x, axis, split_axis=0, concat_axis=0, tiled=True)


def on_device(
    queries,
    key_heads,
    value_heads,
    doc_ids,
    residual,
    ln_gain,
    expert_ids,
    expert_weight,
    w_gate,
    w_up,
    w_down,
):
    rows = queries.shape[1]
    features = residual.shape[2]
    ctx_count = lax.axis_size("ctx")
    tp_count = lax.axis_size("tp")
    dp_index = lax.axis_index("dp").reshape(1)
    ctx_index = lax.axis_index("ctx").reshape(1)
    ids = expert_ids[0].T
    weight = expert_weight[0].T
    hidden_units = w_down.shape[1]

    other_chip = [(i, i ^ 2) for i in range(4)]
    other_core = [(i, i ^ 1) for i in range(4)]
    down = w_down[0]
    both = call(
        stack_kernel,
        jax.ShapeDtypeStruct((2,) + down.shape, BF),
        [ANY, ANY],
        [pltpu.VMEM((2,) + down.shape, BF), pltpu.SemaphoreType.DMA((2,)), pltpu.SemaphoreType.DMA((2,))],
        out_spec=ANY,
        limit=FULL,
        name="stack",
    )(w_gate[0].T, w_up[0].T)
    both_chip = lax.ppermute(both, "dp", other_chip)

    v_first = rows - 16
    docs_row = jnp.broadcast_to(doc_ids.astype(BF), (8, rows))
    packed = jnp.concatenate([key_heads[0], value_heads[0, :v_first], docs_row], axis=0)
    rest = all_to_all(jnp.broadcast_to(value_heads[:, v_first:], (ctx_count, rows - v_first, HEAD_DIM)), "ctx")
    kv = lax.all_gather(packed, "ctx", axis=0)
    back = -(-(REACH - 1) // rows)
    group = queries.shape[2] // HEAD_DIM
    block = -(-(features // 128 * CAP + 5) // 8) * 8
    post, outgoing = call(
        functools.partial(attend_kernel, back, v_first),
        (jax.ShapeDtypeStruct((rows, features), F32), jax.ShapeDtypeStruct((ctx_count, block, 128), BF)),
        [SMEM] + [VMEM] * 6,
        [pltpu.VMEM((back + 1, group * rows, rows), F32)],
        name="attend",
    )(ctx_index, queries[0], kv, rest, doc_ids[0].astype(F32).reshape(rows, 1), residual[0], ids)
    outgoing, down, both, both_chip = lax.optimization_barrier((outgoing, down, both, both_chip))
    landed = all_to_all(outgoing, "ctx")
    down_chip = lax.ppermute(down, "dp", other_chip)
    both_core = lax.ppermute(both, "dp", other_core)
    both_far = lax.ppermute(both_chip, "dp", other_core)
    down_core = lax.ppermute(down, "dp", other_core)
    total_rows = ctx_count * CAP
    copies = call(
        spread_kernel,
        jax.ShapeDtypeStruct((tp_count, total_rows + 16, features), BF),
        [VMEM] * 2,
        [pltpu.VMEM((total_rows + 16, features), F32)],
        name="spread",
    )(landed, ln_gain.reshape(1, features))
    copies, down_chip = lax.optimization_barrier((copies, down_chip))
    arrived = all_to_all(copies, "tp")
    down_far = lax.ppermute(down_chip, "dp", other_core)
    partial = call(
        expert_kernel,
        jax.ShapeDtypeStruct((tp_count, total_rows, features), BF),
        [SMEM] + [ANY] * 9,
        [
            pltpu.VMEM((tp_count, total_rows, features), BF),
            pltpu.VMEM((tp_count, 16, features), BF),
            pltpu.VMEM((4, 3) + down.shape, BF),
            pltpu.VMEM((total_rows, hidden_units), F32),
            pltpu.VMEM((total_rows, hidden_units), F32),
            pltpu.VMEM((total_rows, hidden_units), BF),
            pltpu.VMEM((total_rows, 128), F32),
            pltpu.VMEM((tp_count, total_rows, features), BF),
            pltpu.SemaphoreType.DMA((4, 3)),
            pltpu.SemaphoreType.DMA((17,)),
        ],
        out_spec=ANY,
        limit=FULL,
        flops=6 * total_rows * hidden_units * features * tp_count,
        moved=24 << 20,
        name="expert",
    )(dp_index, arrived, both, both_core, both_chip, both_far, down, down_core, down_chip, down_far)
    block = -(-(features // 128 * CAP) // 8) * 8

    def weigh(term, ids):
        return call(
            functools.partial(weigh_kernel, term),
            jax.ShapeDtypeStruct((ctx_count, block, features), BF),
            [VMEM] * 2,
            name="weigh",
        )(ids, weight)

    partial, ids_later = lax.optimization_barrier((partial, ids))
    groups = all_to_all(partial, "tp")
    upper, lower = weigh(0, ids_later), weigh(1, ids_later)
    groups, upper, lower = lax.optimization_barrier((groups, upper, lower))
    expert_out = call(
        total_kernel,
        jax.ShapeDtypeStruct((ctx_count, block, 128), BF),
        [VMEM],
        [pltpu.VMEM((total_rows, features), F32)],
        name="total",
    )(groups)
    returned = all_to_all(expert_out, "ctx")
    mixed = call(
        combine_kernel,
        jax.ShapeDtypeStruct((rows, features), BF),
        [VMEM] * 4,
        name="combine",
    )(post, upper, lower, returned)
    return mixed[None]


def solution(mesh):
    placed = (
        P("dp", "ctx", "tp"),
        P("dp", "ctx", "tp"),
        P("dp", "ctx", "tp"),
        P("dp", "ctx"),
        P("dp", "ctx", "tp"),
        P("tp"),
        P("dp", "ctx", None),
        P("dp", "ctx", None),
        P("ctx", "dp", "tp"),
        P("ctx", "dp", "tp"),
        P("ctx", "tp", "dp"),
    )
    return jax.shard_map(
        on_device, mesh=mesh, in_specs=placed, out_specs=P("dp", "ctx", "tp"), check_vma=False
    )
```

time: 263 us -> 229 us (0.87)
  the two profiles are of different devices: /device:TPU:64 before, /device:TPU:12 now
where the time goes in v2:
time: 229 us; the launch traced here: 228 us
  blocking collectives  73.9 us (32%)
  waiting for transfers between devices  70.2 us (31%)
  starting transfers between devices  55.4 us (24%)
  Pallas kernels  25.1 us (11%)
  local copies, waits for them, and re-layouts  2.91 us (1%)
    all_to_all x4, waiting for transfers between devices, all_to_all(): return lax.all_to_all(x, axis, split_axis=0, concat_axis=0, tiled=True)  66.6 us
    all_to_all x4, starting transfers between devices, all_to_all(): return lax.all_to_all(x, axis, split_axis=0, concat_axis=0, tiled=True)  40.8 us
    all_to_all x1, blocking collectives, all_to_all(): return lax.all_to_all(x, axis, split_axis=0, concat_axis=0, tiled=True)  37.4 us
    all_gather x1, blocking collectives, on_device(): kv = lax.all_gather(packed, 'ctx', axis=0)  36.5 us
    pallas_call x1, Pallas kernels, on_device(): call(expert_kernel, jax.ShapeDtypeStruct((tp_count, total_rows, features)...  13.8 us
  transfers between devices with their start and end apart: 10, of which 5 were waited for; matrix products, arithmetic and copies ran while one was open for 0% of the time, Pallas kernels for 3%

profile of v2, /device:TPU:12, one launch (start us, length us, event | category | flops | bytes accessed | tf_op | source)
XLA Modules:
  0.0 227.8 jit_solution(4709003661977941991)
XLA Ops:
  0.0 0.0 copy-start.4
  0.0 0.0 copy-start.5
  0.0 0.0 copy-start.6
  0.0 2.7 %stack.1.g0 = bf16[2,672,768]{2,1,0:T(8,128)(2,1)} custom-call(bf16[672,768]{1,0:T(8,128)(2,1)} %bitcast.36, bf16[672,768]{1,0:T(8,128)(2,1)} %bitcast.37), custom_call_target="tpu_custom_call" | custom-call | tf_op jit(solution)/shard_map/stack/pallas_call | solution.py:318
  2.7 0.0 copy-start.12
  2.8 0.0 copy-start.11
  2.8 3.2 %collective-permute-start = (bf16[2,672,768]{2,1,0:T(8,128)(2,1)}, bf16[2,672,768]{2,1,0:T(8,128)(2,1)}, u32[]{:S(2)}, u32[]{:S(2)}) collective-permute-start(bf16[2,672,768]{2,1,0:T(8,128)(2,1)} %stack.1.g0), channel_id=1, source_target_pairs={{0,256},{128,384},{256,0},{384,128},{1,257},{129,385},{257,1},{385... | collective-permute-start | bytes 6193160 | tf_op jit(solution)/shard_map/ppermute | solution.py:327
  6.0 0.0 copy-done.9
  6.0 0.6 broadcast_in_dim.20
  6.7 15.2 %all-to-all-start = ((bf16[16,16,128]{2,1,0:T(8,128)(2,1)}), bf16[16,16,128]{2,1,0:T(8,128)(2,1)S(1)}, u32[]{:S(2)}, u32[]{:S(2)}) async-start(bf16[16,16,128]{2,1,0:T(8,128)(2,1)} %broadcast_in_dim.20), calls=%async_computation | async-start | bytes 131072 | tf_op jit(solution)/shard_map/all_to_all | solution.py:289
  21.9 0.0 copy-done.13
  21.9 0.1 copy.12.docs_ref
  22.0 0.0 copy-done.10
  22.1 36.5 %all-gather = bf16[3968,128]{1,0:T(8,128)(2,1)S(1)} all-gather(bf16[248,128]{1,0:T(8,128)(2,1)S(1)} %pad_maximum_fusion), channel_id=2, replica_groups=mesh['dp'=4,'ctx'=16,'tp'=8] {'ctx'}, dimensions={0}, use_global_device_ids=true | all-gather | bytes 1079296 | tf_op jit(solution)/shard_map/all_gather | solution.py:333
  58.5 0.0 all-to-all-done.rest_ref
  58.5 0.0 copy-done.4
  58.5 0.0 copy-done.5
  58.6 0.0 copy-done.6
  58.6 2.6 %attend.1 = (f32[128,384]{1,0:T(8,128)S(1)}, bf16[16,104,128]{2,1,0:T(8,128)(2,1)}) custom-call(s32[1]{0:T(128)} %bitcast.place_ref, bf16[128,384]{1,0:T(8,128)(2,1)S(1)} %bitcast.29, bf16[16,248,128]{2,1,0:T(8,128)(2,1)S(1)} %bitcast.28, bf16[16,16,128]{2,1,0:T(8,128)(2,1)S(1)} %all-to-all-done.rest_ref, f32[128,1]{1,0:T(8,128)S(1)} %copy.12.docs_ref, ...), custom_call_target="tpu_custom_call" | custom-call | tf_op jit(solution)/shard_map/attend/pallas_call | solution.py:337
  61.2 0.0 collective-permute-done.g2
  61.2 11.8 %all-to-all-start.1 = ((bf16[16,104,128]{2,1,0:T(8,128)(2,1)}), bf16[16,104,128]{2,1,0:T(8,128)(2,1)S(1)}, u32[]{:S(2)}, u32[]{:S(2)}) async-start(bf16[16,104,128]{2,1,0:T(8,128)(2,1)} %get-tuple-element.20), calls=%async_computation.1 | async-start | bytes 851968 | tf_op jit(solution)/shard_map/all_to_all | solution.py:289
  73.0 0.0 copy-done.12
  73.0 2.7 %collective-permute-start.1 = (bf16[672,768]{1,0:T(8,128)(2,1)S(1)}, bf16[672,768]{1,0:T(8,128)(2,1)}, u32[]{:S(2)}, u32[]{:S(2)}) collective-permute-start(bf16[672,768]{1,0:T(8,128)(2,1)S(1)} %bitcast.40), channel_id=1, source_target_pairs={{0,256},{128,384},{256,0},{384,128},{1,257},{129,385},{257,1},{385... | collective-permute-start | bytes 3096584 | tf_op jit(solution)/shard_map/ppermute | solution.py:346
  75.8 0.0 copy-done.11
  75.8 16.1 %all-to-all-done.1.in_ref = bf16[16,104,128]{2,1,0:T(8,128)(2,1)S(1)} async-done(((bf16[16,104,128]{2,1,0:T(8,128)(2,1)}), bf16[16,104,128]{2,1,0:T(8,128)(2,1)S(1)}, u32[]{:S(2)}, u32[]{:S(2)}) %all-to-all-start.1) | async-done | bytes 426016 | tf_op jit(solution)/shard_map/all_to_all | solution.py:289
  91.9 2.3 %spread.1 = bf16[8,544,384]{2,1,0:T(8,128)(2,1)} custom-call(bf16[16,104,128]{2,1,0:T(8,128)(2,1)S(1)} %all-to-all-done.1.in_ref, f32[1,384]{1,0:T(1,128)S(1)} %reshape.23.gain_ref), custom_call_target="tpu_custom_call" | custom-call | tf_op jit(solution)/shard_map/spread/pallas_call | solution.py:351
  94.3 0.0 collective-permute-done.1.d2
  94.3 7.5 %all-to-all-start.2 = ((bf16[8,544,384]{2,1,0:T(8,128)(2,1)}), bf16[8,544,384]{2,1,0:T(8,128)(2,1)}, u32[]{:S(2)}, u32[]{:S(2)}) async-start(bf16[8,544,384]{2,1,0:T(8,128)(2,1)} %spread.1), calls=%async_computation.2 | async-start | bytes 6684672 | tf_op jit(solution)/shard_map/all_to_all | solution.py:289
  101.7 1.9 collective-permute-start.2
  103.7 2.4 %collective-permute-start.3 = (bf16[2,672,768]{2,1,0:T(8,128)(2,1)}, bf16[2,672,768]{2,1,0:T(8,128)(2,1)}, u32[]{:S(2)}, u32[]{:S(2)}) collective-permute-start(bf16[2,672,768]{2,1,0:T(8,128)(2,1)} %collective-permute-done.g2), channel_id=1, source_target_pairs={{0,128},{128,0},{256,384},{384,256},{1,129},{129,1},{257,385},{385... | collective-permute-start | bytes 6193160 | tf_op jit(solution)/shard_map/ppermute | solution.py:348
  106.1 1.9 collective-permute-start.4
  108.0 2.4 %collective-permute-start.5 = (bf16[672,768]{1,0:T(8,128)(2,1)}, bf16[672,768]{1,0:T(8,128)(2,1)}, u32[]{:S(2)}, u32[]{:S(2)}) collective-permute-start(bf16[672,768]{1,0:T(8,128)(2,1)} %collective-permute-done.1.d2), channel_id=1, source_target_pairs={{0,128},{128,0},{256,384},{384,256},{1,129},{129,1},{257,385},{385... | collective-permute-start | bytes 3096584 | tf_op jit(solution)/shard_map/ppermute | solution.py:360
  110.4 1.9 collective-permute-done.4.d1
  112.3 0.0 collective-permute-done.2.g1
  112.3 0.0 collective-permute-done.3.g3
  112.3 1.7 collective-permute-done.5.d3
  114.0 17.2 %all-to-all-done.2.x_ref = bf16[8,544,384]{2,1,0:T(8,128)(2,1)} async-done(((bf16[8,544,384]{2,1,0:T(8,128)(2,1)}), bf16[8,544,384]{2,1,0:T(8,128)(2,1)}, u32[]{:S(2)}, u32[]{:S(2)}) %all-to-all-start.2) | async-done | bytes 3342368 | tf_op jit(solution)/shard_map/all_to_all | solution.py:289
  131.2 13.8 %expert.1 = bf16[8,528,384]{2,1,0:T(8,128)(2,1)} custom-call(s32[1]{0:T(128)} %bitcast.11.dp_ref, bf16[8,544,384]{2,1,0:T(8,128)(2,1)} %all-to-all-done.2.x_ref, bf16[2,672,768]{2,1,0:T(8,128)(2,1)} %stack.1.g0, bf16[2,672,768]{2,1,0:T(8,128)(2,1)} %collective-permute-done.2.g1, bf16[2,672,768]{2,1,0:T(8,128)(2,1)} %collective-permute-done.g2, ...), custom_call_target="tpu_custom_call" | custom-call | flops 6539968512 | bytes 25165824 | tf_op jit(solution)/shard_map/expert/pallas_call | solution.py:361
  145.1 0.0 copy-start.7
  145.1 6.3 %all-to-all-start.3 = ((bf16[8,528,384]{2,1,0:T(8,128)(2,1)}), bf16[8,528,384]{2,1,0:T(8,128)(2,1)S(1)}, u32[]{:S(2)}, u32[]{:S(2)}) async-start(bf16[8,528,384]{2,1,0:T(8,128)(2,1)} %expert.1), calls=%async_computation.3 | async-start | bytes 6488064 | tf_op jit(solution)/shard_map/all_to_all | solution.py:289
  151.4 0.6 weigh.3.lower_ref
  152.0 1.0 copy-done
  153.1 0.6 weigh.2.upper_ref
  153.7 1.1 copy-done.2
  154.7 33.2 %all-to-all-done.3.in_ref = bf16[8,528,384]{2,1,0:T(8,128)(2,1)S(1)} async-done(((bf16[8,528,384]{2,1,0:T(8,128)(2,1)}), bf16[8,528,384]{2,1,0:T(8,128)(2,1)S(1)}, u32[]{:S(2)}, u32[]{:S(2)}) %all-to-all-start.3) | async-done | bytes 3244064 | tf_op jit(solution)/shard_map/all_to_all | solution.py:289
  187.9 0.8 total.1
  188.7 37.4 %all_to_all.25.back_ref = bf16[16,104,128]{2,1,0:T(8,128)(2,1)S(1)} all-to-all(bf16[16,104,128]{2,1,0:T(8,128)(2,1)S(1)} %total.1), channel_id=1, replica_groups=mesh['dp'=4,'ctx'=16,'tp'=8] {'ctx'}, dimensions={0} | all-to-all | bytes 851968 | tf_op jit(solution)/shard_map/all_to_all | solution.py:289
  226.1 1.7 combine.1
  (18 shorter events, 0.0 us)
Async XLA Ops:
  0.0 6.0 %copy-start.9 = (bf16[1,128,128]{2,1,0:T(8,128)(2,1)S(1)}, bf16[1,128,128]{2,1,0:T(8,128)(2,1)}, u32[]{:S(2)}) copy-start(bf16[1,128,128]{2,1,0:T(8,128)(2,1)} %param.13) | copy-start | bytes 98308
  0.0 21.9 %copy-start.13 = (s32[1,128]{1,0:T(1,128)S(1)}, s32[1,128]{1,0:T(1,128)}, u32[]{:S(2)}) copy-start(s32[1,128]{1,0:T(1,128)} %param.14) | copy-start | bytes 1540
  0.0 22.0 %copy-start.10 = (bf16[1,128,128]{2,1,0:T(8,128)(2,1)S(1)}, bf16[1,128,128]{2,1,0:T(8,128)(2,1)}, u32[]{:S(2)}) copy-start(bf16[1,128,128]{2,1,0:T(8,128)(2,1)} %param.12) | copy-start | bytes 98308
  0.0 58.5 %copy-start.4 = (bf16[1,128,384]{2,1,0:T(8,128)(2,1)S(1)}, bf16[1,128,384]{2,1,0:T(8,128)(2,1)}, u32[]{:S(2)}) copy-start(bf16[1,128,384]{2,1,0:T(8,128)(2,1)} %param.11) | copy-start | bytes 294916
  0.0 58.5 %copy-start.5 = (bf16[1,128,384]{2,1,0:T(8,128)(2,1)S(1)}, bf16[1,128,384]{2,1,0:T(8,128)(2,1)}, u32[]{:S(2)}) copy-start(bf16[1,128,384]{2,1,0:T(8,128)(2,1)} %param.15) | copy-start | bytes 294916
  0.0 58.5 %copy-start.6 = (s32[1,128,4]{1,2,0:T(4,128)S(1)}, s32[1,128,4]{1,2,0:T(4,128)}, u32[]{:S(2)}) copy-start(s32[1,128,4]{1,2,0:T(4,128)} %param.17) | copy-start | bytes 6148
  2.7 70.3 %copy-start.12 = (bf16[1,672,768]{2,1,0:T(8,128)(2,1)S(1)}, bf16[1,672,768]{2,1,0:T(8,128)(2,1)}, u32[]{:S(2)}) copy-start(bf16[1,672,768]{2,1,0:T(8,128)(2,1)} %param.21) | copy-start | bytes 3096580
  2.8 73.0 %copy-start.11 = (f32[384]{0:T(512)S(1)}, f32[384]{0:T(512)}, u32[]{:S(2)}) copy-start(f32[384]{0:T(512)} %param.16) | copy-start | bytes 4612
  2.8 58.4 %collective-permute-start = (bf16[2,672,768]{2,1,0:T(8,128)(2,1)}, bf16[2,672,768]{2,1,0:T(8,128)(2,1)}, u32[]{:S(2)}, u32[]{:S(2)}) collective-permute-start(bf16[2,672,768]{2,1,0:T(8,128)(2,1)} %stack.1.g0), channel_id=1, source_target_pairs={{0,256},{128,384},{256,0},{384,128},{1,257},{129,385},{257,1},{385... | collective-permute-start | bytes 6193160 | tf_op jit(solution)/shard_map/ppermute | solution.py:327
  6.7 51.9 %all-to-all-start = ((bf16[16,16,128]{2,1,0:T(8,128)(2,1)}), bf16[16,16,128]{2,1,0:T(8,128)(2,1)S(1)}, u32[]{:S(2)}, u32[]{:S(2)}) async-start(bf16[16,16,128]{2,1,0:T(8,128)(2,1)} %broadcast_in_dim.20), calls=%async_computation | async-start | bytes 131072 | tf_op jit(solution)/shard_map/all_to_all | solution.py:289
  61.2 30.8 %all-to-all-start.1 = ((bf16[16,104,128]{2,1,0:T(8,128)(2,1)}), bf16[16,104,128]{2,1,0:T(8,128)(2,1)S(1)}, u32[]{:S(2)}, u32[]{:S(2)}) async-start(bf16[16,104,128]{2,1,0:T(8,128)(2,1)} %get-tuple-element.20), calls=%async_computation.1 | async-start | bytes 851968 | tf_op jit(solution)/shard_map/all_to_all | solution.py:289
  73.0 21.2 %collective-permute-start.1 = (bf16[672,768]{1,0:T(8,128)(2,1)S(1)}, bf16[672,768]{1,0:T(8,128)(2,1)}, u32[]{:S(2)}, u32[]{:S(2)}) collective-permute-start(bf16[672,768]{1,0:T(8,128)(2,1)S(1)} %bitcast.40), channel_id=1, source_target_pairs={{0,256},{128,384},{256,0},{384,128},{1,257},{129,385},{257,1},{385... | collective-permute-start | bytes 3096584 | tf_op jit(solution)/shard_map/ppermute | solution.py:346
  94.3 7.5 %copy-start.8 = (bf16[2,672,768]{2,1,0:T(8,128)(2,1)S(1)}, bf16[2,672,768]{2,1,0:T(8,128)(2,1)}, u32[]{:S(2)}) copy-start(bf16[2,672,768]{2,1,0:T(8,128)(2,1)} %stack.1.g0) | copy-start | bytes 6193156
  94.3 36.9 %all-to-all-start.2 = ((bf16[8,544,384]{2,1,0:T(8,128)(2,1)}), bf16[8,544,384]{2,1,0:T(8,128)(2,1)}, u32[]{:S(2)}, u32[]{:S(2)}) async-start(bf16[8,544,384]{2,1,0:T(8,128)(2,1)} %spread.1), calls=%async_computation.2 | async-start | bytes 6684672 | tf_op jit(solution)/shard_map/all_to_all | solution.py:289
  101.7 10.6 %collective-permute-start.2 = (bf16[2,672,768]{2,1,0:T(8,128)(2,1)S(1)}, bf16[2,672,768]{2,1,0:T(8,128)(2,1)}, u32[]{:S(2)}, u32[]{:S(2)}) collective-permute-start(bf16[2,672,768]{2,1,0:T(8,128)(2,1)S(1)} %copy-done.8), channel_id=1, source_target_pairs={{0,128},{128,0},{256,384},{384,256},{1,129},{129,1},{257,385},{385... | collective-permute-start | bytes 6193160 | tf_op jit(solution)/shard_map/ppermute | solution.py:347
  103.7 8.6 %collective-permute-start.3 = (bf16[2,672,768]{2,1,0:T(8,128)(2,1)}, bf16[2,672,768]{2,1,0:T(8,128)(2,1)}, u32[]{:S(2)}, u32[]{:S(2)}) collective-permute-start(bf16[2,672,768]{2,1,0:T(8,128)(2,1)} %collective-permute-done.g2), channel_id=1, source_target_pairs={{0,128},{128,0},{256,384},{384,256},{1,129},{129,1},{257,385},{385... | collective-permute-start | bytes 6193160 | tf_op jit(solution)/shard_map/ppermute | solution.py:348
  106.1 6.2 %collective-permute-start.4 = (bf16[672,768]{1,0:T(8,128)(2,1)S(1)}, bf16[672,768]{1,0:T(8,128)(2,1)}, u32[]{:S(2)}, u32[]{:S(2)}) collective-permute-start(bf16[672,768]{1,0:T(8,128)(2,1)S(1)} %bitcast.41), channel_id=1, source_target_pairs={{0,128},{128,0},{256,384},{384,256},{1,129},{129,1},{257,385},{385... | collective-permute-start | bytes 3096584 | tf_op jit(solution)/shard_map/ppermute | solution.py:349
  108.0 6.0 %collective-permute-start.5 = (bf16[672,768]{1,0:T(8,128)(2,1)}, bf16[672,768]{1,0:T(8,128)(2,1)}, u32[]{:S(2)}, u32[]{:S(2)}) collective-permute-start(bf16[672,768]{1,0:T(8,128)(2,1)} %collective-permute-done.1.d2), channel_id=1, source_target_pairs={{0,128},{128,0},{256,384},{384,256},{1,129},{129,1},{257,385},{385... | collective-permute-start | bytes 3096584 | tf_op jit(solution)/shard_map/ppermute | solution.py:360
  145.1 6.3 %copy-start.7 = (f32[1,128,4]{1,2,0:T(4,128)S(1)}, f32[1,128,4]{1,2,0:T(4,128)}, u32[]{:S(2)}) copy-start(f32[1,128,4]{1,2,0:T(4,128)} %param.18) | copy-start | bytes 6148
  145.1 42.8 %all-to-all-start.3 = ((bf16[8,528,384]{2,1,0:T(8,128)(2,1)}), bf16[8,528,384]{2,1,0:T(8,128)(2,1)S(1)}, u32[]{:S(2)}, u32[]{:S(2)}) async-start(bf16[8,528,384]{2,1,0:T(8,128)(2,1)} %expert.1), calls=%async_computation.3 | async-start | bytes 6488064 | tf_op jit(solution)/shard_map/all_to_all | solution.py:289
  152.0 1.0 copy-start
  153.7 1.1 copy-start.2
  187.9 38.2 %copy-start.1 = (bf16[16,104,384]{2,1,0:T(8,128)(2,1)S(1)}, bf16[16,104,384]{2,1,0:T(8,128)(2,1)}, u32[]{:S(2)}) copy-start(bf16[16,104,384]{2,1,0:T(8,128)(2,1)} %copy-done) | copy-start | bytes 3833860
  187.9 38.2 %copy-start.3 = (bf16[16,104,384]{2,1,0:T(8,128)(2,1)S(1)}, bf16[16,104,384]{2,1,0:T(8,128)(2,1)}, u32[]{:S(2)}) copy-start(bf16[16,104,384]{2,1,0:T(8,128)(2,1)} %copy-done.2) | copy-start | bytes 3833860

commit v3 on v2

--- a/solution.py
+++ b/solution.py
@@ -10,6 +10,7 @@
 
 HEAD_DIM = 128
 CAP = 33
+EXPERTS = 16
 FULL = 58 << 20
 REACH = 1152
 BF = jnp.bfloat16
@@ -48,14 +49,20 @@
     return out
 
 
-def stack_kernel(*refs):
-    *sources, out_ref, held, arrive, leave = refs
-    into = [pltpu.make_async_copy(source, held.at[i], arrive.at[i]) for i, source in enumerate(sources)]
-    away = [pltpu.make_async_copy(held.at[i], out_ref.at[i], leave.at[i]) for i in range(len(sources))]
+def stack_kernel(gate_ref, up_ref, value_ref, both_ref, rest_ref, held, few, arrive, leave):
+    count, rows, _ = rest_ref.shape
+    first = pltpu.make_async_copy(value_ref.at[pl.ds(value_ref.shape[0] - rows, rows), :], few, arrive.at[2])
+    first.start()
+    into = [pltpu.make_async_copy(source, held.at[i], arrive.at[i]) for i, source in enumerate((gate_ref, up_ref))]
+    away = [pltpu.make_async_copy(held.at[i], both_ref.at[i], leave.at[i]) for i in range(2)]
     for copy in into:
         copy.start()
-    for first, then in zip(into, away):
-        first.wait()
+    first.wait()
+    away += [pltpu.make_async_copy(few, rest_ref.at[i], leave.at[2 + i]) for i in range(count)]
+    for copy in away[2:]:
+        copy.start()
+    for one, then in zip(into, away):
+        one.wait()
         then.start()
     for copy in away:
         copy.wait()
@@ -117,21 +124,22 @@
     mean = jnp.mean(post, axis=1, keepdims=True)
     centred = post - mean
     square = jnp.sum(centred * centred, axis=1, keepdims=True)
-    centred = centred.astype(BF)
-    ones = jnp.ones((rows, rows), F32)
-    parts = terms((mean * ones).T[0:1], 3) + terms((square * ones).T[0:1], 2)
-    parts = jnp.concatenate(parts + [jnp.zeros((3, rows), F32)], axis=0).astype(BF)
-    stacked = jnp.concatenate([centred[:, g * lanes : (g + 1) * lanes] for g in range(groups)], axis=0)
+    lane = lax.broadcasted_iota(jnp.int32, (rows, lanes), 1)
+    stats = jnp.zeros((rows, lanes), F32)
+    for q, part in enumerate(terms(mean, 3) + terms(square, 2)):
+        stats = jnp.where(lane == q, part, stats)
+    source = jnp.concatenate([centred.astype(BF), stats.astype(BF)], axis=1)
     rank = named_and_rank(ids_ref, experts).astype(jnp.int32)
-    wanted = jnp.concatenate([rank + g * CAP for g in range(groups)], axis=1)
-    place = lax.broadcasted_iota(jnp.int32, (block, groups * rows), 0)
-    slot = lax.broadcasted_iota(jnp.int32, (lanes, rows), 0)
+    deep = -(-CAP // 8) * 8
+    slot = lax.broadcasted_iota(jnp.int32, (deep, rows), 0)
+    picks = [jnp.where(slot == rank[e : e + 1, :], 1.0, 0.0) for e in range(experts)]
+    found = dot(jnp.concatenate(picks, axis=0).astype(BF), source)
+    turned = found[:, wide:].T[0:8]
     for e in range(experts):
-        pick = jnp.where(place == wanted[e : e + 1, :], 1.0, 0.0).astype(BF)
-        data = dot(pick, stacked)
-        pick = jnp.where(slot == rank[e : e + 1, :], 1.0, 0.0).astype(BF)
-        stats = dot(parts, pick, NT)
-        out_ref[e] = jnp.concatenate([data[: groups * CAP], stats[: block - groups * CAP]], axis=0).astype(BF)
+        mine = slice(e * deep, e * deep + CAP)
+        runs = [found[mine, g * lanes : (g + 1) * lanes] for g in range(groups)]
+        numbers = jnp.concatenate([turned[:, e * deep : (e + 1) * deep], jnp.zeros((8, lanes - deep), F32)], axis=1)
+        out_ref[e] = jnp.concatenate(runs + [numbers[: block - groups * CAP]], axis=0).astype(BF)
 
 
 def spread_kernel(in_ref, gain_ref, out_ref, flat):
@@ -248,7 +256,7 @@
     total = in_ref[0].astype(F32)
     for p in range(1, parts):
         total = total + in_ref[p].astype(F32)
-    flat[...] = total
+    flat[0 : total.shape[0], :] = total
     groups = features // lanes
     for b in range(blocks):
         block = flat[b * CAP : (b + 1) * CAP, :]
@@ -258,29 +266,32 @@
 
 
 def weigh_kernel(term, ids_ref, weight_ref, out_ref):
-    experts, rows, wide = out_ref.shape
+    wide, places = out_ref.shape
     tokens = ids_ref.shape[1]
     groups = wide // tokens
-    rank = named_and_rank(ids_ref, experts).astype(jnp.int32)
+    experts = EXPERTS
+    block = places // experts
+    rank = named_and_rank(ids_ref, experts)
     expert = lax.broadcasted_iota(jnp.int32, (experts, tokens), 0)
     weight = jnp.zeros((experts, tokens), F32)
     for k in range(ids_ref.shape[0]):
         weight = weight + jnp.where(ids_ref[k : k + 1, :] == expert, weight_ref[k : k + 1, :], 0.0)
     weight = terms(weight, 2)[term]
-    wide_rank = jnp.concatenate([rank + g * CAP for g in range(groups)], axis=1)
-    wide_weight = jnp.concatenate([weight] * groups, axis=1)
-    row = lax.broadcasted_iota(jnp.int32, (rows, wide), 0)
-    for e in range(experts):
-        out_ref[e] = jnp.where(row == wide_rank[e : e + 1, :], wide_weight[e : e + 1, :], 0.0).astype(BF)
+    place = lax.broadcasted_iota(jnp.int32, (experts, places), 1)
+    start = lax.broadcasted_iota(jnp.int32, (experts, places), 0) * block
+    own = jnp.where((place >= start) & (place < start + block), 1.0, 0.0).astype(BF)
+    rank = dot(rank.astype(BF), own, TN)
+    weight = dot(weight.astype(BF), own, TN)
+    at = lax.rem(lax.broadcasted_iota(jnp.int32, (tokens, places), 1), block).astype(F32)
+    for g in range(groups):
+        out_ref[g * tokens : (g + 1) * tokens, :] = jnp.where(at == rank + g * CAP, weight, 0.0).astype(BF)
 
 
 def combine_kernel(post_ref, upper_ref, lower_ref, back_ref, out_ref):
     tokens, features = post_ref.shape
-    experts, rows, lanes = back_ref.shape
-    groups = features // lanes
-    moe = jnp.zeros((groups * tokens, lanes), F32)
-    for e in range(experts):
-        moe = moe + dot(upper_ref[e], back_ref[e], TN) + dot(lower_ref[e], back_ref[e], TN)
+    groups = features // back_ref.shape[1]
+    back = back_ref[...]
+    moe = dot(upper_ref[...], back) + dot(lower_ref[...], back)
     moe = jnp.concatenate([moe[g * tokens : (g + 1) * tokens] for g in range(groups)], axis=1)
     out_ref[...] = (post_ref[...] + moe).astype(BF)
 
@@ -315,21 +326,29 @@
     other_chip = [(i, i ^ 2) for i in range(4)]
     other_core = [(i, i ^ 1) for i in range(4)]
     down = w_down[0]
-    both = call(
+    v_first = rows - 16
+    both, rest = call(
         stack_kernel,
-        jax.ShapeDtypeStruct((2,) + down.shape, BF),
-        [ANY, ANY],
-        [pltpu.VMEM((2,) + down.shape, BF), pltpu.SemaphoreType.DMA((2,)), pltpu.SemaphoreType.DMA((2,))],
+        (
+            jax.ShapeDtypeStruct((2,) + down.shape, BF),
+            jax.ShapeDtypeStruct((ctx_count, rows - v_first, HEAD_DIM), BF),
+        ),
+        [ANY] * 3,
+        [
+            pltpu.VMEM((2,) + down.shape, BF),
+            pltpu.VMEM((rows - v_first, HEAD_DIM), BF),
+            pltpu.SemaphoreType.DMA((3,)),
+            pltpu.SemaphoreType.DMA((2 + ctx_count,)),
+        ],
         out_spec=ANY,
         limit=FULL,
         name="stack",
-    )(w_gate[0].T, w_up[0].T)
+    )(w_gate[0].T, w_up[0].T, value_heads[0])
     both_chip = lax.ppermute(both, "dp", other_chip)
 
-    v_first = rows - 16
     docs_row = jnp.broadcast_to(doc_ids.astype(BF), (8, rows))
     packed = jnp.concatenate([key_heads[0], value_heads[0, :v_first], docs_row], axis=0)
-    rest = all_to_all(jnp.broadcast_to(value_heads[:, v_first:], (ctx_count, rows - v_first, HEAD_DIM)), "ctx")
+    rest = all_to_all(rest, "ctx")
     kv = lax.all_gather(packed, "ctx", axis=0)
     back = -(-(REACH - 1) // rows)
     group = queries.shape[2] // HEAD_DIM
@@ -385,7 +404,7 @@
     def weigh(term, ids):
         return call(
             functools.partial(weigh_kernel, term),
-            jax.ShapeDtypeStruct((ctx_count, block, features), BF),
+            jax.ShapeDtypeStruct((features, ctx_count * block), BF),
             [VMEM] * 2,
             name="weigh",
         )(ids, weight)
@@ -398,7 +417,7 @@
         total_kernel,
         jax.ShapeDtypeStruct((ctx_count, block, 128), BF),
         [VMEM],
-        [pltpu.VMEM((total_rows, features), F32)],
+        [pltpu.VMEM((total_rows + 16, features), F32)],
         name="total",
     )(groups)
     returned = all_to_all(expert_out, "ctx")
@@ -407,7 +426,7 @@
         jax.ShapeDtypeStruct((rows, features), BF),
         [VMEM] * 4,
         name="combine",
-    )(post, upper, lower, returned)
+    )(post, upper, lower, returned.reshape(ctx_count * block, 128))
     return mixed[None]
 
 

time: 229 us -> 229 us (level)
  the two profiles are of different devices: /device:TPU:12 before, /device:TPU:14 now
where the time goes in v3:
time: 229 us; the launch traced here: 228 us
  blocking collectives  73.2 us (32%)
  waiting for transfers between devices  71.9 us (31%)
  starting transfers between devices  55.5 us (24%)
  Pallas kernels  24.8 us (11%)
    all_to_all x4, waiting for transfers between devices, all_to_all(): return lax.all_to_all(x, axis, split_axis=0, concat_axis=0, tiled=True)  68.4 us
    all_to_all x4, starting transfers between devices, all_to_all(): return lax.all_to_all(x, axis, split_axis=0, concat_axis=0, tiled=True)  40.9 us
    all_to_all x1, blocking collectives, all_to_all(): return lax.all_to_all(x, axis, split_axis=0, concat_axis=0, tiled=True)  36.7 us
    all_gather x1, blocking collectives, on_device(): kv = lax.all_gather(packed, 'ctx', axis=0)  36.5 us
    pallas_call x1, Pallas kernels, on_device(): call(expert_kernel, jax.ShapeDtypeStruct((tp_count, total_rows, features)...  13.9 us
  transfers between devices with their start and end apart: 10, of which 5 were waited for; matrix products, arithmetic and copies ran while one was open for 0% of the time, Pallas kernels for 3%

profile of v3, /device:TPU:14, one launch (start us, length us, event | category | flops | bytes accessed | tf_op | source)
XLA Modules:
  0.0 228.0 jit_solution(18113409053361184831)
XLA Ops:
  0.0 0.0 copy-start.6
  0.0 0.0 copy-start.5
  0.0 0.0 copy-start.4
  0.0 2.9 %stack.1 = (bf16[2,672,768]{2,1,0:T(8,128)(2,1)}, bf16[16,16,128]{2,1,0:T(8,128)(2,1)}) custom-call(bf16[672,768]{1,0:T(8,128)(2,1)} %bitcast.37, bf16[672,768]{1,0:T(8,128)(2,1)} %bitcast.38, bf16[128,128]{1,0:T(8,128)(2,1)} %bitcast.39), custom_call_target="tpu_custom_call" | custom-call | tf_op jit(solution)/shard_map/stack/pallas_call | solution.py:330
  2.9 0.0 copy-start.12
  2.9 0.0 copy-start.10
  3.0 2.9 %collective-permute-start = (bf16[2,672,768]{2,1,0:T(8,128)(2,1)}, bf16[2,672,768]{2,1,0:T(8,128)(2,1)}, u32[]{:S(2)}, u32[]{:S(2)}) collective-permute-start(bf16[2,672,768]{2,1,0:T(8,128)(2,1)} %get-tuple-element.27.g0), channel_id=1, source_target_pairs={{0,256},{128,384},{256,0},{384,128},{1,257},{129,385},{257,1},{385... | collective-permute-start | bytes 6193160 | tf_op jit(solution)/shard_map/ppermute | solution.py:347
  5.8 15.2 %all-to-all-start = ((bf16[16,16,128]{2,1,0:T(8,128)(2,1)}), bf16[16,16,128]{2,1,0:T(8,128)(2,1)S(1)}, u32[]{:S(2)}, u32[]{:S(2)}) async-start(bf16[16,16,128]{2,1,0:T(8,128)(2,1)} %get-tuple-element.20), calls=%async_computation | async-start | bytes 131072 | tf_op jit(solution)/shard_map/all_to_all | solution.py:300
  21.1 0.0 copy-done.13
  21.1 0.1 copy.12.docs_ref
  21.2 0.0 copy-done.8
  21.2 0.0 copy-done.9
  21.2 36.5 %all-gather = bf16[3968,128]{1,0:T(8,128)(2,1)S(1)} all-gather(bf16[248,128]{1,0:T(8,128)(2,1)S(1)} %pad_maximum_fusion), channel_id=2, replica_groups=mesh['dp'=4,'ctx'=16,'tp'=8] {'ctx'}, dimensions={0}, use_global_device_ids=true | all-gather | bytes 1079296 | tf_op jit(solution)/shard_map/all_gather | solution.py:352
  57.7 0.0 all-to-all-done.rest_ref
  57.7 0.0 copy-done.4
  57.7 2.1 attend.1
  59.8 0.0 collective-permute-done.g2
  59.8 11.9 %all-to-all-start.1 = ((bf16[16,104,128]{2,1,0:T(8,128)(2,1)}), bf16[16,104,128]{2,1,0:T(8,128)(2,1)S(1)}, u32[]{:S(2)}, u32[]{:S(2)}) async-start(bf16[16,104,128]{2,1,0:T(8,128)(2,1)} %get-tuple-element.24), calls=%async_computation.1 | async-start | bytes 851968 | tf_op jit(solution)/shard_map/all_to_all | solution.py:300
  71.7 0.0 copy-done.12
  71.7 3.1 %collective-permute-start.1 = (bf16[672,768]{1,0:T(8,128)(2,1)S(1)}, bf16[672,768]{1,0:T(8,128)(2,1)}, u32[]{:S(2)}, u32[]{:S(2)}) collective-permute-start(bf16[672,768]{1,0:T(8,128)(2,1)S(1)} %bitcast.42), channel_id=1, source_target_pairs={{0,256},{128,384},{256,0},{384,128},{1,257},{129,385},{257,1},{385... | collective-permute-start | bytes 3096584 | tf_op jit(solution)/shard_map/ppermute | solution.py:365
  74.9 15.5 %all-to-all-done.1.in_ref = bf16[16,104,128]{2,1,0:T(8,128)(2,1)S(1)} async-done(((bf16[16,104,128]{2,1,0:T(8,128)(2,1)}), bf16[16,104,128]{2,1,0:T(8,128)(2,1)S(1)}, u32[]{:S(2)}, u32[]{:S(2)}) %all-to-all-start.1) | async-done | bytes 426016 | tf_op jit(solution)/shard_map/all_to_all | solution.py:300
  90.3 2.3 %spread.1 = bf16[8,544,384]{2,1,0:T(8,128)(2,1)} custom-call(bf16[16,104,128]{2,1,0:T(8,128)(2,1)S(1)} %all-to-all-done.1.in_ref, f32[1,384]{1,0:T(1,128)S(1)} %reshape.26.gain_ref), custom_call_target="tpu_custom_call" | custom-call | tf_op jit(solution)/shard_map/spread/pallas_call | solution.py:370
  92.6 0.0 collective-permute-done.1.d2
  92.6 7.5 %all-to-all-start.2 = ((bf16[8,544,384]{2,1,0:T(8,128)(2,1)}), bf16[8,544,384]{2,1,0:T(8,128)(2,1)}, u32[]{:S(2)}, u32[]{:S(2)}) async-start(bf16[8,544,384]{2,1,0:T(8,128)(2,1)} %spread.1), calls=%async_computation.2 | async-start | bytes 6684672 | tf_op jit(solution)/shard_map/all_to_all | solution.py:300
  100.1 1.9 collective-permute-start.2
  102.0 2.4 %collective-permute-start.3 = (bf16[2,672,768]{2,1,0:T(8,128)(2,1)}, bf16[2,672,768]{2,1,0:T(8,128)(2,1)}, u32[]{:S(2)}, u32[]{:S(2)}) collective-permute-start(bf16[2,672,768]{2,1,0:T(8,128)(2,1)} %collective-permute-done.g2), channel_id=1, source_target_pairs={{0,128},{128,0},{256,384},{384,256},{1,129},{129,1},{257,385},{385... | collective-permute-start | bytes 6193160 | tf_op jit(solution)/shard_map/ppermute | solution.py:367
  104.4 1.9 collective-permute-start.4
  106.4 2.4 %collective-permute-start.5 = (bf16[672,768]{1,0:T(8,128)(2,1)}, bf16[672,768]{1,0:T(8,128)(2,1)}, u32[]{:S(2)}, u32[]{:S(2)}) collective-permute-start(bf16[672,768]{1,0:T(8,128)(2,1)} %collective-permute-done.1.d2), channel_id=1, source_target_pairs={{0,128},{128,0},{256,384},{384,256},{1,129},{129,1},{257,385},{385... | collective-permute-start | bytes 3096584 | tf_op jit(solution)/shard_map/ppermute | solution.py:379
  108.8 1.9 collective-permute-done.4.d1
  110.7 0.0 collective-permute-done.2.g1
  110.7 0.0 collective-permute-done.3.g3
  110.7 1.7 collective-permute-done.5.d3
  112.3 19.3 %all-to-all-done.2.x_ref = bf16[8,544,384]{2,1,0:T(8,128)(2,1)} async-done(((bf16[8,544,384]{2,1,0:T(8,128)(2,1)}), bf16[8,544,384]{2,1,0:T(8,128)(2,1)}, u32[]{:S(2)}, u32[]{:S(2)}) %all-to-all-start.2) | async-done | bytes 3342368 | tf_op jit(solution)/shard_map/all_to_all | solution.py:300
  131.6 13.9 %expert.1 = bf16[8,528,384]{2,1,0:T(8,128)(2,1)} custom-call(s32[1]{0:T(128)} %bitcast.15.dp_ref, bf16[8,544,384]{2,1,0:T(8,128)(2,1)} %all-to-all-done.2.x_ref, bf16[2,672,768]{2,1,0:T(8,128)(2,1)} %get-tuple-element.27.g0, bf16[2,672,768]{2,1,0:T(8,128)(2,1)} %collective-permute-done.2.g1, bf16[2,672,768]{2,1,0:T(8,128)(2,1)} %collective-permute-done.g2, ...), custom_call_target="tpu_custom_call" | custom-call | flops 6539968512 | bytes 25165824 | tf_op jit(solution)/shard_map/expert/pallas_call | solution.py:380
  145.5 0.0 copy-start.7
  145.5 6.3 %all-to-all-start.3 = ((bf16[8,528,384]{2,1,0:T(8,128)(2,1)}), bf16[8,528,384]{2,1,0:T(8,128)(2,1)S(1)}, u32[]{:S(2)}, u32[]{:S(2)}) async-start(bf16[8,528,384]{2,1,0:T(8,128)(2,1)} %expert.1), calls=%async_computation.3 | async-start | bytes 6488064 | tf_op jit(solution)/shard_map/all_to_all | solution.py:300
  151.8 0.0 copy-done.7
  151.8 0.7 weigh.3.lower_ref
  152.5 0.0 copy-start
  152.5 1.0 copy-done
  153.6 0.7 weigh.2.upper_ref
  154.3 0.0 copy-start.2
  154.3 1.0 copy-done.2
  155.3 33.6 %all-to-all-done.3.in_ref = bf16[8,528,384]{2,1,0:T(8,128)(2,1)S(1)} async-done(((bf16[8,528,384]{2,1,0:T(8,128)(2,1)}), bf16[8,528,384]{2,1,0:T(8,128)(2,1)S(1)}, u32[]{:S(2)}, u32[]{:S(2)}) %all-to-all-start.3) | async-done | bytes 3244064 | tf_op jit(solution)/shard_map/all_to_all | solution.py:300
  189.0 0.8 total.1
  189.8 36.7 %all_to_all.25 = bf16[16,104,128]{2,1,0:T(8,128)(2,1)S(1)} all-to-all(bf16[16,104,128]{2,1,0:T(8,128)(2,1)S(1)} %total.1), channel_id=1, replica_groups=mesh['dp'=4,'ctx'=16,'tp'=8] {'ctx'}, dimensions={0} | all-to-all | bytes 851968 | tf_op jit(solution)/shard_map/all_to_all | solution.py:300
  226.5 0.0 copy-done.1
  226.5 1.5 combine.1
  (16 shorter events, 0.0 us)
Async XLA Ops:
  0.0 21.2 %copy-start.8 = (bf16[1,128,128]{2,1,0:T(8,128)(2,1)S(1)}, bf16[1,128,128]{2,1,0:T(8,128)(2,1)}, u32[]{:S(2)}) copy-start(bf16[1,128,128]{2,1,0:T(8,128)(2,1)} %param.13) | copy-start | bytes 98308
  0.0 21.1 %copy-start.13 = (s32[1,128]{1,0:T(1,128)S(1)}, s32[1,128]{1,0:T(1,128)}, u32[]{:S(2)}) copy-start(s32[1,128]{1,0:T(1,128)} %param.14) | copy-start | bytes 1540
  0.0 21.2 %copy-start.9 = (bf16[1,128,128]{2,1,0:T(8,128)(2,1)S(1)}, bf16[1,128,128]{2,1,0:T(8,128)(2,1)}, u32[]{:S(2)}) copy-start(bf16[1,128,128]{2,1,0:T(8,128)(2,1)} %param.12) | copy-start | bytes 98308
  0.0 57.7 %copy-start.6 = (s32[1,128,4]{1,2,0:T(4,128)S(1)}, s32[1,128,4]{1,2,0:T(4,128)}, u32[]{:S(2)}) copy-start(s32[1,128,4]{1,2,0:T(4,128)} %param.17) | copy-start | bytes 6148
  0.0 57.7 %copy-start.5 = (bf16[1,128,384]{2,1,0:T(8,128)(2,1)S(1)}, bf16[1,128,384]{2,1,0:T(8,128)(2,1)}, u32[]{:S(2)}) copy-start(bf16[1,128,384]{2,1,0:T(8,128)(2,1)} %param.15) | copy-start | bytes 294916
  0.0 57.7 %copy-start.4 = (bf16[1,128,384]{2,1,0:T(8,128)(2,1)S(1)}, bf16[1,128,384]{2,1,0:T(8,128)(2,1)}, u32[]{:S(2)}) copy-start(bf16[1,128,384]{2,1,0:T(8,128)(2,1)} %param.11) | copy-start | bytes 294916
  2.9 68.8 %copy-start.12 = (bf16[1,672,768]{2,1,0:T(8,128)(2,1)S(1)}, bf16[1,672,768]{2,1,0:T(8,128)(2,1)}, u32[]{:S(2)}) copy-start(bf16[1,672,768]{2,1,0:T(8,128)(2,1)} %param.21) | copy-start | bytes 3096580
  2.9 71.9 %copy-start.10 = (f32[384]{0:T(512)S(1)}, f32[384]{0:T(512)}, u32[]{:S(2)}) copy-start(f32[384]{0:T(512)} %param.16) | copy-start | bytes 4612
  3.0 56.9 %collective-permute-start = (bf16[2,672,768]{2,1,0:T(8,128)(2,1)}, bf16[2,672,768]{2,1,0:T(8,128)(2,1)}, u32[]{:S(2)}, u32[]{:S(2)}) collective-permute-start(bf16[2,672,768]{2,1,0:T(8,128)(2,1)} %get-tuple-element.27.g0), channel_id=1, source_target_pairs={{0,256},{128,384},{256,0},{384,128},{1,257},{129,385},{257,1},{385... | collective-permute-start | bytes 6193160 | tf_op jit(solution)/shard_map/ppermute | solution.py:347
  5.8 51.9 %all-to-all-start = ((bf16[16,16,128]{2,1,0:T(8,128)(2,1)}), bf16[16,16,128]{2,1,0:T(8,128)(2,1)S(1)}, u32[]{:S(2)}, u32[]{:S(2)}) async-start(bf16[16,16,128]{2,1,0:T(8,128)(2,1)} %get-tuple-element.20), calls=%async_computation | async-start | bytes 131072 | tf_op jit(solution)/shard_map/all_to_all | solution.py:300
  59.8 30.5 %all-to-all-start.1 = ((bf16[16,104,128]{2,1,0:T(8,128)(2,1)}), bf16[16,104,128]{2,1,0:T(8,128)(2,1)S(1)}, u32[]{:S(2)}, u32[]{:S(2)}) async-start(bf16[16,104,128]{2,1,0:T(8,128)(2,1)} %get-tuple-element.24), calls=%async_computation.1 | async-start | bytes 851968 | tf_op jit(solution)/shard_map/all_to_all | solution.py:300
  71.7 20.9 %collective-permute-start.1 = (bf16[672,768]{1,0:T(8,128)(2,1)S(1)}, bf16[672,768]{1,0:T(8,128)(2,1)}, u32[]{:S(2)}, u32[]{:S(2)}) collective-permute-start(bf16[672,768]{1,0:T(8,128)(2,1)S(1)} %bitcast.42), channel_id=1, source_target_pairs={{0,256},{128,384},{256,0},{384,128},{1,257},{129,385},{257,1},{385... | collective-permute-start | bytes 3096584 | tf_op jit(solution)/shard_map/ppermute | solution.py:365
  92.6 7.5 %copy-start.11 = (bf16[2,672,768]{2,1,0:T(8,128)(2,1)S(1)}, bf16[2,672,768]{2,1,0:T(8,128)(2,1)}, u32[]{:S(2)}) copy-start(bf16[2,672,768]{2,1,0:T(8,128)(2,1)} %get-tuple-element.27.g0) | copy-start | bytes 6193156
  92.6 39.0 %all-to-all-start.2 = ((bf16[8,544,384]{2,1,0:T(8,128)(2,1)}), bf16[8,544,384]{2,1,0:T(8,128)(2,1)}, u32[]{:S(2)}, u32[]{:S(2)}) async-start(bf16[8,544,384]{2,1,0:T(8,128)(2,1)} %spread.1), calls=%async_computation.2 | async-start | bytes 6684672 | tf_op jit(solution)/shard_map/all_to_all | solution.py:300
  100.1 10.6 %collective-permute-start.2 = (bf16[2,672,768]{2,1,0:T(8,128)(2,1)S(1)}, bf16[2,672,768]{2,1,0:T(8,128)(2,1)}, u32[]{:S(2)}, u32[]{:S(2)}) collective-permute-start(bf16[2,672,768]{2,1,0:T(8,128)(2,1)S(1)} %copy-done.11), channel_id=1, source_target_pairs={{0,128},{128,0},{256,384},{384,256},{1,129},{129,1},{257,385},{385... | collective-permute-start | bytes 6193160 | tf_op jit(solution)/shard_map/ppermute | solution.py:366
  102.0 8.6 %collective-permute-start.3 = (bf16[2,672,768]{2,1,0:T(8,128)(2,1)}, bf16[2,672,768]{2,1,0:T(8,128)(2,1)}, u32[]{:S(2)}, u32[]{:S(2)}) collective-permute-start(bf16[2,672,768]{2,1,0:T(8,128)(2,1)} %collective-permute-done.g2), channel_id=1, source_target_pairs={{0,128},{128,0},{256,384},{384,256},{1,129},{129,1},{257,385},{385... | collective-permute-start | bytes 6193160 | tf_op jit(solution)/shard_map/ppermute | solution.py:367
  104.4 6.2 %collective-permute-start.4 = (bf16[672,768]{1,0:T(8,128)(2,1)S(1)}, bf16[672,768]{1,0:T(8,128)(2,1)}, u32[]{:S(2)}, u32[]{:S(2)}) collective-permute-start(bf16[672,768]{1,0:T(8,128)(2,1)S(1)} %bitcast.43), channel_id=1, source_target_pairs={{0,128},{128,0},{256,384},{384,256},{1,129},{129,1},{257,385},{385... | collective-permute-start | bytes 3096584 | tf_op jit(solution)/shard_map/ppermute | solution.py:368
  106.4 6.0 %collective-permute-start.5 = (bf16[672,768]{1,0:T(8,128)(2,1)}, bf16[672,768]{1,0:T(8,128)(2,1)}, u32[]{:S(2)}, u32[]{:S(2)}) collective-permute-start(bf16[672,768]{1,0:T(8,128)(2,1)} %collective-permute-done.1.d2), channel_id=1, source_target_pairs={{0,128},{128,0},{256,384},{384,256},{1,129},{129,1},{257,385},{385... | collective-permute-start | bytes 3096584 | tf_op jit(solution)/shard_map/ppermute | solution.py:379
  145.5 6.3 %copy-start.7 = (f32[1,128,4]{1,2,0:T(4,128)S(1)}, f32[1,128,4]{1,2,0:T(4,128)}, u32[]{:S(2)}) copy-start(f32[1,128,4]{1,2,0:T(4,128)} %param.18) | copy-start | bytes 6148
  145.5 43.5 %all-to-all-start.3 = ((bf16[8,528,384]{2,1,0:T(8,128)(2,1)}), bf16[8,528,384]{2,1,0:T(8,128)(2,1)S(1)}, u32[]{:S(2)}, u32[]{:S(2)}) async-start(bf16[8,528,384]{2,1,0:T(8,128)(2,1)} %expert.1), calls=%async_computation.3 | async-start | bytes 6488064 | tf_op jit(solution)/shard_map/all_to_all | solution.py:300
  152.5 1.0 copy-start
  154.3 1.1 copy-start.2
  189.0 37.5 %copy-start.1 = (bf16[384,1664]{1,0:T(8,128)(2,1)S(1)}, bf16[384,1664]{1,0:T(8,128)(2,1)}, u32[]{:S(2)}) copy-start(bf16[384,1664]{1,0:T(8,128)(2,1)} %copy-done) | copy-start | bytes 3833860
  189.0 37.5 %copy-start.3 = (bf16[384,1664]{1,0:T(8,128)(2,1)S(1)}, bf16[384,1664]{1,0:T(8,128)(2,1)}, u32[]{:S(2)}) copy-start(bf16[384,1664]{1,0:T(8,128)(2,1)} %copy-done.2) | copy-start | bytes 3833860

commit v4 on v3

--- a/solution.py
+++ b/solution.py
@@ -217,20 +217,21 @@
         arriving["x", p, i].wait()
         return ((x_in[2 * p + i].astype(F32) + shift) * scale * gain).astype(BF)
 
-    for p in range(4):
-        x = jnp.concatenate([normed(p, 0), normed(p, 1)], axis=1)
-        arriving[p, 0].wait()
-        arriving[p, 1].wait()
-        if p < 2:
-            begin(*piece(p + 2))
-        else:
-            begin((2 * p - 4, 2), (2 * p - 3, 2))
-        g = dot(x, held[p, 0], NT)
-        u = dot(x, held[p, 1], NT)
-        if p == 0:
+    for now in ((0,), (1,), (2, 3)):
+        x = [jnp.concatenate([normed(p, 0), normed(p, 1)], axis=1) for p in now]
+        for p in now:
+            arriving[p, 0].wait()
+            arriving[p, 1].wait()
+        if now[0] < 2:
+            begin(*piece(now[0] + 2))
+        if now[0] > 0:
+            begin((2 * now[0] - 2, 2), (2 * now[0] - 1, 2))
+        g = sum(dot(part, held[p, 0], NT) for p, part in zip(now, x))
+        u = sum(dot(part, held[p, 1], NT) for p, part in zip(now, x))
+        if now[0] == 0:
             gate[...] = g
             up[...] = u
-        elif p < 3:
+        elif now[0] < 2:
             gate[...] += g
             up[...] += u
         else:
@@ -239,13 +240,17 @@
             hidden[...] = (g / (1.0 + jnp.exp(-g)) * u).astype(BF)
     leaving = []
     for p in range(4):
-        j = dp ^ p
         arriving[p, 2].wait()
-        y = dot(hidden[...], held[p, 2]).astype(BF)
-        for i in range(2):
-            y_out[2 * p + i] = y[:, i * features : (i + 1) * features]
-            leaving.append(pltpu.make_async_copy(y_out.at[2 * p + i], out_ref.at[2 * j + i], more.at[9 + 2 * p + i]))
-            leaving[-1].start()
+    for now in ((0, 1), (2, 3)):
+        for p in now:
+            y = dot(hidden[...], held[p, 2]).astype(BF)
+            for i in range(2):
+                y_out[2 * p + i] = y[:, i * features : (i + 1) * features]
+        for p in now:
+            for i in range(2):
+                target = out_ref.at[2 * (dp ^ p) + i]
+                leaving.append(pltpu.make_async_copy(y_out.at[2 * p + i], target, more.at[9 + 2 * p + i]))
+                leaving[-1].start()
     for copy in leaving:
         copy.wait()
 

time: 229 us -> 228 us (level)
  no operation moved by 1% of the time
where the time goes in v4:
time: 228 us; the launch traced here: 227 us
  blocking collectives  73.2 us (32%)
  waiting for transfers between devices  71.9 us (32%)
  starting transfers between devices  55.5 us (24%)
  Pallas kernels  24.1 us (11%)
    all_to_all x4, waiting for transfers between devices, all_to_all(): return lax.all_to_all(x, axis, split_axis=0, concat_axis=0, tiled=True)  68.4 us
    all_to_all x4, starting transfers between devices, all_to_all(): return lax.all_to_all(x, axis, split_axis=0, concat_axis=0, tiled=True)  40.9 us
    all_to_all x1, blocking collectives, all_to_all(): return lax.all_to_all(x, axis, split_axis=0, concat_axis=0, tiled=True)  36.7 us
    all_gather x1, blocking collectives, on_device(): kv = lax.all_gather(packed, 'ctx', axis=0)  36.5 us
    pallas_call x1, Pallas kernels, on_device(): call(expert_kernel, jax.ShapeDtypeStruct((tp_count, total_rows, features)...  13.2 us
  transfers between devices with their start and end apart: 10, of which 5 were waited for; matrix products, arithmetic and copies ran while one was open for 0% of the time, Pallas kernels for 3%

profile of v4, /device:TPU:14, one launch (start us, length us, event | category | flops | bytes accessed | tf_op | source)
XLA Modules:
  0.0 227.3 jit_solution(6998503943667154546)
XLA Ops:
  0.0 0.0 copy-start.6
  0.0 0.0 copy-start.5
  0.0 0.0 copy-start.4
  0.0 2.9 %stack.1 = (bf16[2,672,768]{2,1,0:T(8,128)(2,1)}, bf16[16,16,128]{2,1,0:T(8,128)(2,1)}) custom-call(bf16[672,768]{1,0:T(8,128)(2,1)} %bitcast.37, bf16[672,768]{1,0:T(8,128)(2,1)} %bitcast.38, bf16[128,128]{1,0:T(8,128)(2,1)} %bitcast.39), custom_call_target="tpu_custom_call" | custom-call | tf_op jit(solution)/shard_map/stack/pallas_call | solution.py:335
  2.9 0.0 copy-start.12
  2.9 0.0 copy-start.10
  3.0 2.9 %collective-permute-start = (bf16[2,672,768]{2,1,0:T(8,128)(2,1)}, bf16[2,672,768]{2,1,0:T(8,128)(2,1)}, u32[]{:S(2)}, u32[]{:S(2)}) collective-permute-start(bf16[2,672,768]{2,1,0:T(8,128)(2,1)} %get-tuple-element.27.g0), channel_id=1, source_target_pairs={{0,256},{128,384},{256,0},{384,128},{1,257},{129,385},{257,1},{385... | collective-permute-start | bytes 6193160 | tf_op jit(solution)/shard_map/ppermute | solution.py:352
  5.8 15.2 %all-to-all-start = ((bf16[16,16,128]{2,1,0:T(8,128)(2,1)}), bf16[16,16,128]{2,1,0:T(8,128)(2,1)S(1)}, u32[]{:S(2)}, u32[]{:S(2)}) async-start(bf16[16,16,128]{2,1,0:T(8,128)(2,1)} %get-tuple-element.20), calls=%async_computation | async-start | bytes 131072 | tf_op jit(solution)/shard_map/all_to_all | solution.py:305
  21.1 0.0 copy-done.13
  21.1 0.1 copy.12.docs_ref
  21.2 0.0 copy-done.8
  21.2 0.0 copy-done.9
  21.2 36.5 %all-gather = bf16[3968,128]{1,0:T(8,128)(2,1)S(1)} all-gather(bf16[248,128]{1,0:T(8,128)(2,1)S(1)} %pad_maximum_fusion), channel_id=2, replica_groups=mesh['dp'=4,'ctx'=16,'tp'=8] {'ctx'}, dimensions={0}, use_global_device_ids=true | all-gather | bytes 1079296 | tf_op jit(solution)/shard_map/all_gather | solution.py:357
  57.7 0.0 all-to-all-done.rest_ref
  57.7 0.0 copy-done.6
  57.7 0.0 copy-done.5
  57.7 2.1 attend.1
  59.8 0.0 collective-permute-done.g2
  59.8 11.9 %all-to-all-start.1 = ((bf16[16,104,128]{2,1,0:T(8,128)(2,1)}), bf16[16,104,128]{2,1,0:T(8,128)(2,1)S(1)}, u32[]{:S(2)}, u32[]{:S(2)}) async-start(bf16[16,104,128]{2,1,0:T(8,128)(2,1)} %get-tuple-element.24), calls=%async_computation.1 | async-start | bytes 851968 | tf_op jit(solution)/shard_map/all_to_all | solution.py:305
  71.7 3.1 %collective-permute-start.1 = (bf16[672,768]{1,0:T(8,128)(2,1)S(1)}, bf16[672,768]{1,0:T(8,128)(2,1)}, u32[]{:S(2)}, u32[]{:S(2)}) collective-permute-start(bf16[672,768]{1,0:T(8,128)(2,1)S(1)} %bitcast.42), channel_id=1, source_target_pairs={{0,256},{128,384},{256,0},{384,128},{1,257},{129,385},{257,1},{385... | collective-permute-start | bytes 3096584 | tf_op jit(solution)/shard_map/ppermute | solution.py:370
  74.8 0.0 copy-done.10
  74.9 15.5 %all-to-all-done.1.in_ref = bf16[16,104,128]{2,1,0:T(8,128)(2,1)S(1)} async-done(((bf16[16,104,128]{2,1,0:T(8,128)(2,1)}), bf16[16,104,128]{2,1,0:T(8,128)(2,1)S(1)}, u32[]{:S(2)}, u32[]{:S(2)}) %all-to-all-start.1) | async-done | bytes 426016 | tf_op jit(solution)/shard_map/all_to_all | solution.py:305
  90.3 2.3 %spread.1 = bf16[8,544,384]{2,1,0:T(8,128)(2,1)} custom-call(bf16[16,104,128]{2,1,0:T(8,128)(2,1)S(1)} %all-to-all-done.1.in_ref, f32[1,384]{1,0:T(1,128)S(1)} %reshape.26.gain_ref), custom_call_target="tpu_custom_call" | custom-call | tf_op jit(solution)/shard_map/spread/pallas_call | solution.py:375
  92.6 0.0 collective-permute-done.1.d2
  92.6 7.5 %all-to-all-start.2 = ((bf16[8,544,384]{2,1,0:T(8,128)(2,1)}), bf16[8,544,384]{2,1,0:T(8,128)(2,1)}, u32[]{:S(2)}, u32[]{:S(2)}) async-start(bf16[8,544,384]{2,1,0:T(8,128)(2,1)} %spread.1), calls=%async_computation.2 | async-start | bytes 6684672 | tf_op jit(solution)/shard_map/all_to_all | solution.py:305
  100.1 0.0 copy-done.11
  100.1 1.9 collective-permute-start.2
  102.0 2.4 %collective-permute-start.3 = (bf16[2,672,768]{2,1,0:T(8,128)(2,1)}, bf16[2,672,768]{2,1,0:T(8,128)(2,1)}, u32[]{:S(2)}, u32[]{:S(2)}) collective-permute-start(bf16[2,672,768]{2,1,0:T(8,128)(2,1)} %collective-permute-done.g2), channel_id=1, source_target_pairs={{0,128},{128,0},{256,384},{384,256},{1,129},{129,1},{257,385},{385... | collective-permute-start | bytes 6193160 | tf_op jit(solution)/shard_map/ppermute | solution.py:372
  104.4 1.9 collective-permute-start.4
  106.4 2.4 %collective-permute-start.5 = (bf16[672,768]{1,0:T(8,128)(2,1)}, bf16[672,768]{1,0:T(8,128)(2,1)}, u32[]{:S(2)}, u32[]{:S(2)}) collective-permute-start(bf16[672,768]{1,0:T(8,128)(2,1)} %collective-permute-done.1.d2), channel_id=1, source_target_pairs={{0,128},{128,0},{256,384},{384,256},{1,129},{129,1},{257,385},{385... | collective-permute-start | bytes 3096584 | tf_op jit(solution)/shard_map/ppermute | solution.py:384
  108.8 1.9 collective-permute-done.4.d1
  110.7 0.0 collective-permute-done.2.g1
  110.7 0.0 collective-permute-done.3.g3
  110.7 1.7 collective-permute-done.5.d3
  112.3 19.3 %all-to-all-done.2.x_ref = bf16[8,544,384]{2,1,0:T(8,128)(2,1)} async-done(((bf16[8,544,384]{2,1,0:T(8,128)(2,1)}), bf16[8,544,384]{2,1,0:T(8,128)(2,1)}, u32[]{:S(2)}, u32[]{:S(2)}) %all-to-all-start.2) | async-done | bytes 3342368 | tf_op jit(solution)/shard_map/all_to_all | solution.py:305
  131.6 13.2 %expert.1 = bf16[8,528,384]{2,1,0:T(8,128)(2,1)} custom-call(s32[1]{0:T(128)} %bitcast.15.dp_ref, bf16[8,544,384]{2,1,0:T(8,128)(2,1)} %all-to-all-done.2.x_ref, bf16[2,672,768]{2,1,0:T(8,128)(2,1)} %get-tuple-element.27.g0, bf16[2,672,768]{2,1,0:T(8,128)(2,1)} %collective-permute-done.2.g1, bf16[2,672,768]{2,1,0:T(8,128)(2,1)} %collective-permute-done.g2, ...), custom_call_target="tpu_custom_call" | custom-call | flops 6539968512 | bytes 25165824 | tf_op jit(solution)/shard_map/expert/pallas_call | solution.py:385
  144.8 0.0 copy-start.7
  144.8 6.3 %all-to-all-start.3 = ((bf16[8,528,384]{2,1,0:T(8,128)(2,1)}), bf16[8,528,384]{2,1,0:T(8,128)(2,1)S(1)}, u32[]{:S(2)}, u32[]{:S(2)}) async-start(bf16[8,528,384]{2,1,0:T(8,128)(2,1)} %expert.1), calls=%async_computation.3 | async-start | bytes 6488064 | tf_op jit(solution)/shard_map/all_to_all | solution.py:305
  151.1 0.7 weigh.3.lower_ref
  151.8 0.0 copy-start
  151.8 1.0 copy-done
  152.9 0.7 weigh.2.upper_ref
  153.6 0.0 copy-start.2
  153.6 1.0 copy-done.2
  154.6 33.6 %all-to-all-done.3.in_ref = bf16[8,528,384]{2,1,0:T(8,128)(2,1)S(1)} async-done(((bf16[8,528,384]{2,1,0:T(8,128)(2,1)}), bf16[8,528,384]{2,1,0:T(8,128)(2,1)S(1)}, u32[]{:S(2)}, u32[]{:S(2)}) %all-to-all-start.3) | async-done | bytes 3244064 | tf_op jit(solution)/shard_map/all_to_all | solution.py:305
  188.3 0.8 total.1
  189.1 36.7 %all_to_all.25 = bf16[16,104,128]{2,1,0:T(8,128)(2,1)S(1)} all-to-all(bf16[16,104,128]{2,1,0:T(8,128)(2,1)S(1)} %total.1), channel_id=1, replica_groups=mesh['dp'=4,'ctx'=16,'tp'=8] {'ctx'}, dimensions={0} | all-to-all | bytes 851968 | tf_op jit(solution)/shard_map/all_to_all | solution.py:305
  225.8 1.5 combine.1
  (16 shorter events, 0.0 us)
Async XLA Ops:
  0.0 21.2 %copy-start.8 = (bf16[1,128,128]{2,1,0:T(8,128)(2,1)S(1)}, bf16[1,128,128]{2,1,0:T(8,128)(2,1)}, u32[]{:S(2)}) copy-start(bf16[1,128,128]{2,1,0:T(8,128)(2,1)} %param.13) | copy-start | bytes 98308
  0.0 21.1 %copy-start.13 = (s32[1,128]{1,0:T(1,128)S(1)}, s32[1,128]{1,0:T(1,128)}, u32[]{:S(2)}) copy-start(s32[1,128]{1,0:T(1,128)} %param.14) | copy-start | bytes 1540
  0.0 21.2 %copy-start.9 = (bf16[1,128,128]{2,1,0:T(8,128)(2,1)S(1)}, bf16[1,128,128]{2,1,0:T(8,128)(2,1)}, u32[]{:S(2)}) copy-start(bf16[1,128,128]{2,1,0:T(8,128)(2,1)} %param.12) | copy-start | bytes 98308
  0.0 57.7 %copy-start.6 = (s32[1,128,4]{1,2,0:T(4,128)S(1)}, s32[1,128,4]{1,2,0:T(4,128)}, u32[]{:S(2)}) copy-start(s32[1,128,4]{1,2,0:T(4,128)} %param.17) | copy-start | bytes 6148
  0.0 57.7 %copy-start.5 = (bf16[1,128,384]{2,1,0:T(8,128)(2,1)S(1)}, bf16[1,128,384]{2,1,0:T(8,128)(2,1)}, u32[]{:S(2)}) copy-start(bf16[1,128,384]{2,1,0:T(8,128)(2,1)} %param.15) | copy-start | bytes 294916
  0.0 57.7 %copy-start.4 = (bf16[1,128,384]{2,1,0:T(8,128)(2,1)S(1)}, bf16[1,128,384]{2,1,0:T(8,128)(2,1)}, u32[]{:S(2)}) copy-start(bf16[1,128,384]{2,1,0:T(8,128)(2,1)} %param.11) | copy-start | bytes 294916
  2.9 68.8 %copy-start.12 = (bf16[1,672,768]{2,1,0:T(8,128)(2,1)S(1)}, bf16[1,672,768]{2,1,0:T(8,128)(2,1)}, u32[]{:S(2)}) copy-start(bf16[1,672,768]{2,1,0:T(8,128)(2,1)} %param.21) | copy-start | bytes 3096580
  2.9 71.9 %copy-start.10 = (f32[384]{0:T(512)S(1)}, f32[384]{0:T(512)}, u32[]{:S(2)}) copy-start(f32[384]{0:T(512)} %param.16) | copy-start | bytes 4612
  3.0 56.9 %collective-permute-start = (bf16[2,672,768]{2,1,0:T(8,128)(2,1)}, bf16[2,672,768]{2,1,0:T(8,128)(2,1)}, u32[]{:S(2)}, u32[]{:S(2)}) collective-permute-start(bf16[2,672,768]{2,1,0:T(8,128)(2,1)} %get-tuple-element.27.g0), channel_id=1, source_target_pairs={{0,256},{128,384},{256,0},{384,128},{1,257},{129,385},{257,1},{385... | collective-permute-start | bytes 6193160 | tf_op jit(solution)/shard_map/ppermute | solution.py:352
  5.8 51.9 %all-to-all-start = ((bf16[16,16,128]{2,1,0:T(8,128)(2,1)}), bf16[16,16,128]{2,1,0:T(8,128)(2,1)S(1)}, u32[]{:S(2)}, u32[]{:S(2)}) async-start(bf16[16,16,128]{2,1,0:T(8,128)(2,1)} %get-tuple-element.20), calls=%async_computation | async-start | bytes 131072 | tf_op jit(solution)/shard_map/all_to_all | solution.py:305
  59.8 30.5 %all-to-all-start.1 = ((bf16[16,104,128]{2,1,0:T(8,128)(2,1)}), bf16[16,104,128]{2,1,0:T(8,128)(2,1)S(1)}, u32[]{:S(2)}, u32[]{:S(2)}) async-start(bf16[16,104,128]{2,1,0:T(8,128)(2,1)} %get-tuple-element.24), calls=%async_computation.1 | async-start | bytes 851968 | tf_op jit(solution)/shard_map/all_to_all | solution.py:305
  71.7 20.9 %collective-permute-start.1 = (bf16[672,768]{1,0:T(8,128)(2,1)S(1)}, bf16[672,768]{1,0:T(8,128)(2,1)}, u32[]{:S(2)}, u32[]{:S(2)}) collective-permute-start(bf16[672,768]{1,0:T(8,128)(2,1)S(1)} %bitcast.42), channel_id=1, source_target_pairs={{0,256},{128,384},{256,0},{384,128},{1,257},{129,385},{257,1},{385... | collective-permute-start | bytes 3096584 | tf_op jit(solution)/shard_map/ppermute | solution.py:370
  92.6 7.5 %copy-start.11 = (bf16[2,672,768]{2,1,0:T(8,128)(2,1)S(1)}, bf16[2,672,768]{2,1,0:T(8,128)(2,1)}, u32[]{:S(2)}) copy-start(bf16[2,672,768]{2,1,0:T(8,128)(2,1)} %get-tuple-element.27.g0) | copy-start | bytes 6193156
  92.6 39.0 %all-to-all-start.2 = ((bf16[8,544,384]{2,1,0:T(8,128)(2,1)}), bf16[8,544,384]{2,1,0:T(8,128)(2,1)}, u32[]{:S(2)}, u32[]{:S(2)}) async-start(bf16[8,544,384]{2,1,0:T(8,128)(2,1)} %spread.1), calls=%async_computation.2 | async-start | bytes 6684672 | tf_op jit(solution)/shard_map/all_to_all | solution.py:305
  100.1 10.6 %collective-permute-start.2 = (bf16[2,672,768]{2,1,0:T(8,128)(2,1)S(1)}, bf16[2,672,768]{2,1,0:T(8,128)(2,1)}, u32[]{:S(2)}, u32[]{:S(2)}) collective-permute-start(bf16[2,672,768]{2,1,0:T(8,128)(2,1)S(1)} %copy-done.11), channel_id=1, source_target_pairs={{0,128},{128,0},{256,384},{384,256},{1,129},{129,1},{257,385},{385... | collective-permute-start | bytes 6193160 | tf_op jit(solution)/shard_map/ppermute | solution.py:371
  102.0 8.6 %collective-permute-start.3 = (bf16[2,672,768]{2,1,0:T(8,128)(2,1)}, bf16[2,672,768]{2,1,0:T(8,128)(2,1)}, u32[]{:S(2)}, u32[]{:S(2)}) collective-permute-start(bf16[2,672,768]{2,1,0:T(8,128)(2,1)} %collective-permute-done.g2), channel_id=1, source_target_pairs={{0,128},{128,0},{256,384},{384,256},{1,129},{129,1},{257,385},{385... | collective-permute-start | bytes 6193160 | tf_op jit(solution)/shard_map/ppermute | solution.py:372
  104.4 6.2 %collective-permute-start.4 = (bf16[672,768]{1,0:T(8,128)(2,1)S(1)}, bf16[672,768]{1,0:T(8,128)(2,1)}, u32[]{:S(2)}, u32[]{:S(2)}) collective-permute-start(bf16[672,768]{1,0:T(8,128)(2,1)S(1)} %bitcast.43), channel_id=1, source_target_pairs={{0,128},{128,0},{256,384},{384,256},{1,129},{129,1},{257,385},{385... | collective-permute-start | bytes 3096584 | tf_op jit(solution)/shard_map/ppermute | solution.py:373
  106.4 6.0 %collective-permute-start.5 = (bf16[672,768]{1,0:T(8,128)(2,1)}, bf16[672,768]{1,0:T(8,128)(2,1)}, u32[]{:S(2)}, u32[]{:S(2)}) collective-permute-start(bf16[672,768]{1,0:T(8,128)(2,1)} %collective-permute-done.1.d2), channel_id=1, source_target_pairs={{0,128},{128,0},{256,384},{384,256},{1,129},{129,1},{257,385},{385... | collective-permute-start | bytes 3096584 | tf_op jit(solution)/shard_map/ppermute | solution.py:384
  144.8 6.3 %copy-start.7 = (f32[1,128,4]{1,2,0:T(4,128)S(1)}, f32[1,128,4]{1,2,0:T(4,128)}, u32[]{:S(2)}) copy-start(f32[1,128,4]{1,2,0:T(4,128)} %param.18) | copy-start | bytes 6148
  144.8 43.5 %all-to-all-start.3 = ((bf16[8,528,384]{2,1,0:T(8,128)(2,1)}), bf16[8,528,384]{2,1,0:T(8,128)(2,1)S(1)}, u32[]{:S(2)}, u32[]{:S(2)}) async-start(bf16[8,528,384]{2,1,0:T(8,128)(2,1)} %expert.1), calls=%async_computation.3 | async-start | bytes 6488064 | tf_op jit(solution)/shard_map/all_to_all | solution.py:305
  151.8 1.0 copy-start
  153.6 1.1 copy-start.2
  188.3 37.5 %copy-start.1 = (bf16[384,1664]{1,0:T(8,128)(2,1)S(1)}, bf16[384,1664]{1,0:T(8,128)(2,1)}, u32[]{:S(2)}) copy-start(bf16[384,1664]{1,0:T(8,128)(2,1)} %copy-done) | copy-start | bytes 3833860
  188.3 37.5 %copy-start.3 = (bf16[384,1664]{1,0:T(8,128)(2,1)S(1)}, bf16[384,1664]{1,0:T(8,128)(2,1)}, u32[]{:S(2)}) copy-start(bf16[384,1664]{1,0:T(8,128)(2,1)} %copy-done.2) | copy-start | bytes 3833860

commit v5 on v4

--- a/solution.py
+++ b/solution.py
@@ -217,23 +217,20 @@
         arriving["x", p, i].wait()
         return ((x_in[2 * p + i].astype(F32) + shift) * scale * gain).astype(BF)
 
-    for now in ((0,), (1,), (2, 3)):
+    for now in ((0,), (1, 2, 3)):
         x = [jnp.concatenate([normed(p, 0), normed(p, 1)], axis=1) for p in now]
         for p in now:
             arriving[p, 0].wait()
             arriving[p, 1].wait()
-        if now[0] < 2:
-            begin(*piece(now[0] + 2))
-        if now[0] > 0:
-            begin((2 * now[0] - 2, 2), (2 * now[0] - 1, 2))
+        if now[0] == 0:
+            begin(*piece(2), *piece(3))
+        else:
+            begin((0, 2), (1, 2), (2, 2), (3, 2))
         g = sum(dot(part, held[p, 0], NT) for p, part in zip(now, x))
         u = sum(dot(part, held[p, 1], NT) for p, part in zip(now, x))
         if now[0] == 0:
             gate[...] = g
             up[...] = u
-        elif now[0] < 2:
-            gate[...] += g
-            up[...] += u
         else:
             g = gate[...] + g
             u = up[...] + u

time: 228 us -> 230 us (level)
  Pallas kernels: 24.1 us -> 26.6 us
    pallas_call x1, Pallas kernels: 13.2 us -> 15.7 us  [on_device(): call(expert_kernel, jax.ShapeDtypeStruct((tp_count, total_rows, features)...]
where the time goes in v5:
time: 230 us
  blocking collectives  73.2 us (32%)
  waiting for transfers between devices  71.9 us (31%)
  starting transfers between devices  55.5 us (24%)
  Pallas kernels  26.6 us (12%)
    all_to_all x4, waiting for transfers between devices, all_to_all(): return lax.all_to_all(x, axis, split_axis=0, concat_axis=0, tiled=True)  68.4 us
    all_to_all x4, starting transfers between devices, all_to_all(): return lax.all_to_all(x, axis, split_axis=0, concat_axis=0, tiled=True)  40.9 us
    all_to_all x1, blocking collectives, all_to_all(): return lax.all_to_all(x, axis, split_axis=0, concat_axis=0, tiled=True)  36.7 us
    all_gather x1, blocking collectives, on_device(): kv = lax.all_gather(packed, 'ctx', axis=0)  36.5 us
    pallas_call x1, Pallas kernels, on_device(): call(expert_kernel, jax.ShapeDtypeStruct((tp_count, total_rows, features)...  15.7 us
  transfers between devices with their start and end apart: 10, of which 5 were waited for; matrix products, arithmetic and copies ran while one was open for 0% of the time, Pallas kernels for 3%

profile of v5, /device:TPU:14, one launch (start us, length us, event | category | flops | bytes accessed | tf_op | source)
XLA Modules:
  0.0 229.8 jit_solution(3234611252719625098)
XLA Ops:
  0.0 0.0 copy-start.6
  0.0 0.0 copy-start.5
  0.0 0.0 copy-start.4
  0.0 2.9 %stack.1 = (bf16[2,672,768]{2,1,0:T(8,128)(2,1)}, bf16[16,16,128]{2,1,0:T(8,128)(2,1)}) custom-call(bf16[672,768]{1,0:T(8,128)(2,1)} %bitcast.37, bf16[672,768]{1,0:T(8,128)(2,1)} %bitcast.38, bf16[128,128]{1,0:T(8,128)(2,1)} %bitcast.39), custom_call_target="tpu_custom_call" | custom-call | tf_op jit(solution)/shard_map/stack/pallas_call | solution.py:332
  2.9 0.0 copy-start.12
  2.9 0.0 copy-start.10
  3.0 2.9 %collective-permute-start = (bf16[2,672,768]{2,1,0:T(8,128)(2,1)}, bf16[2,672,768]{2,1,0:T(8,128)(2,1)}, u32[]{:S(2)}, u32[]{:S(2)}) collective-permute-start(bf16[2,672,768]{2,1,0:T(8,128)(2,1)} %get-tuple-element.27.g0), channel_id=1, source_target_pairs={{0,256},{128,384},{256,0},{384,128},{1,257},{129,385},{257,1},{385... | collective-permute-start | bytes 6193160 | tf_op jit(solution)/shard_map/ppermute | solution.py:349
  5.8 15.2 %all-to-all-start = ((bf16[16,16,128]{2,1,0:T(8,128)(2,1)}), bf16[16,16,128]{2,1,0:T(8,128)(2,1)S(1)}, u32[]{:S(2)}, u32[]{:S(2)}) async-start(bf16[16,16,128]{2,1,0:T(8,128)(2,1)} %get-tuple-element.20), calls=%async_computation | async-start | bytes 131072 | tf_op jit(solution)/shard_map/all_to_all | solution.py:302
  21.1 0.0 copy-done.13
  21.1 0.1 copy.12.docs_ref
  21.2 0.0 copy-done.8
  21.2 0.0 copy-done.9
  21.2 36.5 %all-gather = bf16[3968,128]{1,0:T(8,128)(2,1)S(1)} all-gather(bf16[248,128]{1,0:T(8,128)(2,1)S(1)} %pad_maximum_fusion), channel_id=2, replica_groups=mesh['dp'=4,'ctx'=16,'tp'=8] {'ctx'}, dimensions={0}, use_global_device_ids=true | all-gather | bytes 1079296 | tf_op jit(solution)/shard_map/all_gather | solution.py:354
  57.7 0.0 all-to-all-done.rest_ref
  57.7 0.0 copy-done.6
  57.7 0.0 copy-done.5
  57.7 0.0 copy-done.4
  57.7 2.1 attend.1
  59.8 0.0 collective-permute-done.g2
  59.8 11.9 %all-to-all-start.1 = ((bf16[16,104,128]{2,1,0:T(8,128)(2,1)}), bf16[16,104,128]{2,1,0:T(8,128)(2,1)S(1)}, u32[]{:S(2)}, u32[]{:S(2)}) async-start(bf16[16,104,128]{2,1,0:T(8,128)(2,1)} %get-tuple-element.24), calls=%async_computation.1 | async-start | bytes 851968 | tf_op jit(solution)/shard_map/all_to_all | solution.py:302
  71.7 0.0 copy-done.12
  71.7 3.1 %collective-permute-start.1 = (bf16[672,768]{1,0:T(8,128)(2,1)S(1)}, bf16[672,768]{1,0:T(8,128)(2,1)}, u32[]{:S(2)}, u32[]{:S(2)}) collective-permute-start(bf16[672,768]{1,0:T(8,128)(2,1)S(1)} %bitcast.42), channel_id=1, source_target_pairs={{0,256},{128,384},{256,0},{384,128},{1,257},{129,385},{257,1},{385... | collective-permute-start | bytes 3096584 | tf_op jit(solution)/shard_map/ppermute | solution.py:367
  74.9 15.5 %all-to-all-done.1.in_ref = bf16[16,104,128]{2,1,0:T(8,128)(2,1)S(1)} async-done(((bf16[16,104,128]{2,1,0:T(8,128)(2,1)}), bf16[16,104,128]{2,1,0:T(8,128)(2,1)S(1)}, u32[]{:S(2)}, u32[]{:S(2)}) %all-to-all-start.1) | async-done | bytes 426016 | tf_op jit(solution)/shard_map/all_to_all | solution.py:302
  90.3 2.3 %spread.1 = bf16[8,544,384]{2,1,0:T(8,128)(2,1)} custom-call(bf16[16,104,128]{2,1,0:T(8,128)(2,1)S(1)} %all-to-all-done.1.in_ref, f32[1,384]{1,0:T(1,128)S(1)} %reshape.26.gain_ref), custom_call_target="tpu_custom_call" | custom-call | tf_op jit(solution)/shard_map/spread/pallas_call | solution.py:372
  92.6 0.0 collective-permute-done.1.d2
  92.6 7.5 %all-to-all-start.2 = ((bf16[8,544,384]{2,1,0:T(8,128)(2,1)}), bf16[8,544,384]{2,1,0:T(8,128)(2,1)}, u32[]{:S(2)}, u32[]{:S(2)}) async-start(bf16[8,544,384]{2,1,0:T(8,128)(2,1)} %spread.1), calls=%async_computation.2 | async-start | bytes 6684672 | tf_op jit(solution)/shard_map/all_to_all | solution.py:302
  100.1 1.9 collective-permute-start.2
  102.0 2.4 %collective-permute-start.3 = (bf16[2,672,768]{2,1,0:T(8,128)(2,1)}, bf16[2,672,768]{2,1,0:T(8,128)(2,1)}, u32[]{:S(2)}, u32[]{:S(2)}) collective-permute-start(bf16[2,672,768]{2,1,0:T(8,128)(2,1)} %collective-permute-done.g2), channel_id=1, source_target_pairs={{0,128},{128,0},{256,384},{384,256},{1,129},{129,1},{257,385},{385... | collective-permute-start | bytes 6193160 | tf_op jit(solution)/shard_map/ppermute | solution.py:369
  104.4 1.9 collective-permute-start.4
  106.4 2.4 %collective-permute-start.5 = (bf16[672,768]{1,0:T(8,128)(2,1)}, bf16[672,768]{1,0:T(8,128)(2,1)}, u32[]{:S(2)}, u32[]{:S(2)}) collective-permute-start(bf16[672,768]{1,0:T(8,128)(2,1)} %collective-permute-done.1.d2), channel_id=1, source_target_pairs={{0,128},{128,0},{256,384},{384,256},{1,129},{129,1},{257,385},{385... | collective-permute-start | bytes 3096584 | tf_op jit(solution)/shard_map/ppermute | solution.py:381
  108.8 1.9 collective-permute-done.4.d1
  110.7 0.0 collective-permute-done.2.g1
  110.7 0.0 collective-permute-done.3.g3
  110.7 1.7 collective-permute-done.5.d3
  112.3 19.3 %all-to-all-done.2.x_ref = bf16[8,544,384]{2,1,0:T(8,128)(2,1)} async-done(((bf16[8,544,384]{2,1,0:T(8,128)(2,1)}), bf16[8,544,384]{2,1,0:T(8,128)(2,1)}, u32[]{:S(2)}, u32[]{:S(2)}) %all-to-all-start.2) | async-done | bytes 3342368 | tf_op jit(solution)/shard_map/all_to_all | solution.py:302
  131.6 15.7 %expert.1 = bf16[8,528,384]{2,1,0:T(8,128)(2,1)} custom-call(s32[1]{0:T(128)} %bitcast.15.dp_ref, bf16[8,544,384]{2,1,0:T(8,128)(2,1)} %all-to-all-done.2.x_ref, bf16[2,672,768]{2,1,0:T(8,128)(2,1)} %get-tuple-element.27.g0, bf16[2,672,768]{2,1,0:T(8,128)(2,1)} %collective-permute-done.2.g1, bf16[2,672,768]{2,1,0:T(8,128)(2,1)} %collective-permute-done.g2, ...), custom_call_target="tpu_custom_call" | custom-call | flops 6539968512 | bytes 25165824 | tf_op jit(solution)/shard_map/expert/pallas_call | solution.py:382
  147.3 0.0 copy-start.7
  147.3 6.3 %all-to-all-start.3 = ((bf16[8,528,384]{2,1,0:T(8,128)(2,1)}), bf16[8,528,384]{2,1,0:T(8,128)(2,1)S(1)}, u32[]{:S(2)}, u32[]{:S(2)}) async-start(bf16[8,528,384]{2,1,0:T(8,128)(2,1)} %expert.1), calls=%async_computation.3 | async-start | bytes 6488064 | tf_op jit(solution)/shard_map/all_to_all | solution.py:302
  153.6 0.0 copy-done.7
  153.6 0.7 weigh.3.lower_ref
  154.3 1.0 copy-done
  155.4 0.7 weigh.2.upper_ref
  156.1 1.0 copy-done.2
  157.1 33.6 %all-to-all-done.3.in_ref = bf16[8,528,384]{2,1,0:T(8,128)(2,1)S(1)} async-done(((bf16[8,528,384]{2,1,0:T(8,128)(2,1)}), bf16[8,528,384]{2,1,0:T(8,128)(2,1)S(1)}, u32[]{:S(2)}, u32[]{:S(2)}) %all-to-all-start.3) | async-done | bytes 3244064 | tf_op jit(solution)/shard_map/all_to_all | solution.py:302
  190.8 0.8 total.1
  191.6 36.7 %all_to_all.25 = bf16[16,104,128]{2,1,0:T(8,128)(2,1)S(1)} all-to-all(bf16[16,104,128]{2,1,0:T(8,128)(2,1)S(1)} %total.1), channel_id=1, replica_groups=mesh['dp'=4,'ctx'=16,'tp'=8] {'ctx'}, dimensions={0} | all-to-all | bytes 851968 | tf_op jit(solution)/shard_map/all_to_all | solution.py:302
  228.3 0.0 copy-done.3
  228.3 1.5 combine.1
  (16 shorter events, 0.0 us)
Async XLA Ops:
  0.0 21.2 %copy-start.8 = (bf16[1,128,128]{2,1,0:T(8,128)(2,1)S(1)}, bf16[1,128,128]{2,1,0:T(8,128)(2,1)}, u32[]{:S(2)}) copy-start(bf16[1,128,128]{2,1,0:T(8,128)(2,1)} %param.13) | copy-start | bytes 98308
  0.0 21.1 %copy-start.13 = (s32[1,128]{1,0:T(1,128)S(1)}, s32[1,128]{1,0:T(1,128)}, u32[]{:S(2)}) copy-start(s32[1,128]{1,0:T(1,128)} %param.14) | copy-start | bytes 1540
  0.0 21.2 %copy-start.9 = (bf16[1,128,128]{2,1,0:T(8,128)(2,1)S(1)}, bf16[1,128,128]{2,1,0:T(8,128)(2,1)}, u32[]{:S(2)}) copy-start(bf16[1,128,128]{2,1,0:T(8,128)(2,1)} %param.12) | copy-start | bytes 98308
  0.0 57.7 %copy-start.6 = (s32[1,128,4]{1,2,0:T(4,128)S(1)}, s32[1,128,4]{1,2,0:T(4,128)}, u32[]{:S(2)}) copy-start(s32[1,128,4]{1,2,0:T(4,128)} %param.17) | copy-start | bytes 6148
  0.0 57.7 %copy-start.5 = (bf16[1,128,384]{2,1,0:T(8,128)(2,1)S(1)}, bf16[1,128,384]{2,1,0:T(8,128)(2,1)}, u32[]{:S(2)}) copy-start(bf16[1,128,384]{2,1,0:T(8,128)(2,1)} %param.15) | copy-start | bytes 294916
  0.0 57.7 %copy-start.4 = (bf16[1,128,384]{2,1,0:T(8,128)(2,1)S(1)}, bf16[1,128,384]{2,1,0:T(8,128)(2,1)}, u32[]{:S(2)}) copy-start(bf16[1,128,384]{2,1,0:T(8,128)(2,1)} %param.11) | copy-start | bytes 294916
  2.9 68.8 %copy-start.12 = (bf16[1,672,768]{2,1,0:T(8,128)(2,1)S(1)}, bf16[1,672,768]{2,1,0:T(8,128)(2,1)}, u32[]{:S(2)}) copy-start(bf16[1,672,768]{2,1,0:T(8,128)(2,1)} %param.21) | copy-start | bytes 3096580
  2.9 71.9 %copy-start.10 = (f32[384]{0:T(512)S(1)}, f32[384]{0:T(512)}, u32[]{:S(2)}) copy-start(f32[384]{0:T(512)} %param.16) | copy-start | bytes 4612
  3.0 56.9 %collective-permute-start = (bf16[2,672,768]{2,1,0:T(8,128)(2,1)}, bf16[2,672,768]{2,1,0:T(8,128)(2,1)}, u32[]{:S(2)}, u32[]{:S(2)}) collective-permute-start(bf16[2,672,768]{2,1,0:T(8,128)(2,1)} %get-tuple-element.27.g0), channel_id=1, source_target_pairs={{0,256},{128,384},{256,0},{384,128},{1,257},{129,385},{257,1},{385... | collective-permute-start | bytes 6193160 | tf_op jit(solution)/shard_map/ppermute | solution.py:349
  5.8 51.9 %all-to-all-start = ((bf16[16,16,128]{2,1,0:T(8,128)(2,1)}), bf16[16,16,128]{2,1,0:T(8,128)(2,1)S(1)}, u32[]{:S(2)}, u32[]{:S(2)}) async-start(bf16[16,16,128]{2,1,0:T(8,128)(2,1)} %get-tuple-element.20), calls=%async_computation | async-start | bytes 131072 | tf_op jit(solution)/shard_map/all_to_all | solution.py:302
  59.8 30.5 %all-to-all-start.1 = ((bf16[16,104,128]{2,1,0:T(8,128)(2,1)}), bf16[16,104,128]{2,1,0:T(8,128)(2,1)S(1)}, u32[]{:S(2)}, u32[]{:S(2)}) async-start(bf16[16,104,128]{2,1,0:T(8,128)(2,1)} %get-tuple-element.24), calls=%async_computation.1 | async-start | bytes 851968 | tf_op jit(solution)/shard_map/all_to_all | solution.py:302
  71.7 20.9 %collective-permute-start.1 = (bf16[672,768]{1,0:T(8,128)(2,1)S(1)}, bf16[672,768]{1,0:T(8,128)(2,1)}, u32[]{:S(2)}, u32[]{:S(2)}) collective-permute-start(bf16[672,768]{1,0:T(8,128)(2,1)S(1)} %bitcast.42), channel_id=1, source_target_pairs={{0,256},{128,384},{256,0},{384,128},{1,257},{129,385},{257,1},{385... | collective-permute-start | bytes 3096584 | tf_op jit(solution)/shard_map/ppermute | solution.py:367
  92.6 7.5 %copy-start.11 = (bf16[2,672,768]{2,1,0:T(8,128)(2,1)S(1)}, bf16[2,672,768]{2,1,0:T(8,128)(2,1)}, u32[]{:S(2)}) copy-start(bf16[2,672,768]{2,1,0:T(8,128)(2,1)} %get-tuple-element.27.g0) | copy-start | bytes 6193156
  92.6 39.0 %all-to-all-start.2 = ((bf16[8,544,384]{2,1,0:T(8,128)(2,1)}), bf16[8,544,384]{2,1,0:T(8,128)(2,1)}, u32[]{:S(2)}, u32[]{:S(2)}) async-start(bf16[8,544,384]{2,1,0:T(8,128)(2,1)} %spread.1), calls=%async_computation.2 | async-start | bytes 6684672 | tf_op jit(solution)/shard_map/all_to_all | solution.py:302
  100.1 10.6 %collective-permute-start.2 = (bf16[2,672,768]{2,1,0:T(8,128)(2,1)S(1)}, bf16[2,672,768]{2,1,0:T(8,128)(2,1)}, u32[]{:S(2)}, u32[]{:S(2)}) collective-permute-start(bf16[2,672,768]{2,1,0:T(8,128)(2,1)S(1)} %copy-done.11), channel_id=1, source_target_pairs={{0,128},{128,0},{256,384},{384,256},{1,129},{129,1},{257,385},{385... | collective-permute-start | bytes 6193160 | tf_op jit(solution)/shard_map/ppermute | solution.py:368
  102.0 8.6 %collective-permute-start.3 = (bf16[2,672,768]{2,1,0:T(8,128)(2,1)}, bf16[2,672,768]{2,1,0:T(8,128)(2,1)}, u32[]{:S(2)}, u32[]{:S(2)}) collective-permute-start(bf16[2,672,768]{2,1,0:T(8,128)(2,1)} %collective-permute-done.g2), channel_id=1, source_target_pairs={{0,128},{128,0},{256,384},{384,256},{1,129},{129,1},{257,385},{385... | collective-permute-start | bytes 6193160 | tf_op jit(solution)/shard_map/ppermute | solution.py:369
  104.4 6.2 %collective-permute-start.4 = (bf16[672,768]{1,0:T(8,128)(2,1)S(1)}, bf16[672,768]{1,0:T(8,128)(2,1)}, u32[]{:S(2)}, u32[]{:S(2)}) collective-permute-start(bf16[672,768]{1,0:T(8,128)(2,1)S(1)} %bitcast.43), channel_id=1, source_target_pairs={{0,128},{128,0},{256,384},{384,256},{1,129},{129,1},{257,385},{385... | collective-permute-start | bytes 3096584 | tf_op jit(solution)/shard_map/ppermute | solution.py:370
  106.4 6.0 %collective-permute-start.5 = (bf16[672,768]{1,0:T(8,128)(2,1)}, bf16[672,768]{1,0:T(8,128)(2,1)}, u32[]{:S(2)}, u32[]{:S(2)}) collective-permute-start(bf16[672,768]{1,0:T(8,128)(2,1)} %collective-permute-done.1.d2), channel_id=1, source_target_pairs={{0,128},{128,0},{256,384},{384,256},{1,129},{129,1},{257,385},{385... | collective-permute-start | bytes 3096584 | tf_op jit(solution)/shard_map/ppermute | solution.py:381
  147.3 6.3 %copy-start.7 = (f32[1,128,4]{1,2,0:T(4,128)S(1)}, f32[1,128,4]{1,2,0:T(4,128)}, u32[]{:S(2)}) copy-start(f32[1,128,4]{1,2,0:T(4,128)} %param.18) | copy-start | bytes 6148
  147.3 43.5 %all-to-all-start.3 = ((bf16[8,528,384]{2,1,0:T(8,128)(2,1)}), bf16[8,528,384]{2,1,0:T(8,128)(2,1)S(1)}, u32[]{:S(2)}, u32[]{:S(2)}) async-start(bf16[8,528,384]{2,1,0:T(8,128)(2,1)} %expert.1), calls=%async_computation.3 | async-start | bytes 6488064 | tf_op jit(solution)/shard_map/all_to_all | solution.py:302
  154.3 1.0 copy-start
  156.1 1.1 copy-start.2
  190.8 37.5 %copy-start.1 = (bf16[384,1664]{1,0:T(8,128)(2,1)S(1)}, bf16[384,1664]{1,0:T(8,128)(2,1)}, u32[]{:S(2)}) copy-start(bf16[384,1664]{1,0:T(8,128)(2,1)} %copy-done) | copy-start | bytes 3833860
  190.8 37.5 %copy-start.3 = (bf16[384,1664]{1,0:T(8,128)(2,1)S(1)}, bf16[384,1664]{1,0:T(8,128)(2,1)}, u32[]{:S(2)}) copy-start(bf16[384,1664]{1,0:T(8,128)(2,1)} %copy-done.2) | copy-start | bytes 3833860
